TPU v7x, 256 devices: a whole 4x4x8 slice. The times are simulated.
256 devices in a mesh: seq: 64 (over x, z, core), head: 4 (over y).
Axes of the slice: x: 4, y: 4, z: 8, core: 2. Of those that a mesh axis runs over, the one named last changes fastest.
Arguments:
- att_q: bfloat16 [8192, 2048], P('seq', 'head'), may hold values from -120 to 120
- att_k: bfloat16 [8192, 2048], P('seq', 'head'), may hold values from -4 to 4
- att_v: bfloat16 [8192, 2048], P('seq', 'head'), may hold values from -6 to 6
- att_dy: bfloat16 [8192, 2048], P('seq', 'head'), may hold values from -6 to 6
- att_out_w: bfloat16 [2048, 2048], P('head'), may hold values from -0.125 to 0.125
- gdn_q: bfloat16 [8192, 2048], P('seq', 'head'), may hold values from -0.5 to 0.5
- gdn_k: bfloat16 [8192, 2048], P('seq', 'head'), may hold values from -1 to 1, as said below
- gdn_v: bfloat16 [8192, 2048], P('seq', 'head'), may hold values from -6 to 6
- gdn_beta: float32 [16, 8192], P('head', 'seq'), may hold values from 0.001 to 0.95
- gdn_gate: float32 [16, 8192], P('head', 'seq'), may hold values from -3 to 0
- gdn_state: float32 [64, 16, 128, 128], P('seq', 'head'), may hold values from -1.5 to 1.5
- gdn_dy: bfloat16 [8192, 2048], P('seq', 'head'), may hold values from -3 to 3
- gdn_out_w: bfloat16 [2048, 2048], P('head'), may hold values from -0.125 to 0.125
Outputs:
- att_dq: bfloat16 [8192, 2048], P('seq', 'head')
- att_dk: bfloat16 [8192, 2048], P('seq', 'head')
- att_dv: bfloat16 [8192, 2048], P('seq', 'head')
- gdn_dq: bfloat16 [8192, 2048], P('seq', 'head')
- gdn_dk: bfloat16 [8192, 2048], P('seq', 'head')
- gdn_dv: bfloat16 [8192, 2048], P('seq', 'head')
- gdn_dbeta: float32 [16, 8192], P('head', 'seq')
- gdn_dgate: float32 [16, 8192], P('head', 'seq')
Inputs may be any that keep to these rules, and one draw needn't show every extreme that they name: `gdn_k`: the 128 features of one head for one token form a vector of length one, up to rounding.
All inputs are finite; a program needn't handle non-finite values.
Results may differ from a plain program's by a relative error of at most 0.014.
Values may be sent and summed in bfloat16 or wider, within the bound.
No kernel may reach another device: no remote copies, remote signals or barrier semaphores. Data moves between devices by JAX's collectives and lax.ppermute only.
A program may use at most 192 MiB of HBM per device.

v0:
```python
import math

import jax
import jax.numpy as jnp
from jax import lax
from jax.sharding import PartitionSpec as P

HD = 128
WINDOW = 1024
GROUP = 64
DOCS = 2


def passed_along(value, axis, steps):
    count = lax.axis_size(axis)
    initial, last = (max(0, -steps), min(count, count - steps))
    return lax.ppermute(value, axis, [(source, source + steps) for source in range(initial, last)])


def exact_dot(left, right):
    return jnp.dot(left, right, precision=lax.Precision.HIGHEST)


def group_terms(key_rows, beta_rates, gate_log):
    size_c = key_rows.shape[0]
    cum_log = jnp.cumsum(gate_log)
    growth = jnp.exp(cum_log)
    row_ids = jnp.arange(size_c)[:, None]
    col_ids = jnp.arange(size_c)[None, :]
    decays = jnp.where(
        row_ids >= col_ids, jnp.exp(jnp.minimum(cum_log[:, None] - cum_log[None, :], 0.0)), 0.0
    )
    key_gram = exact_dot(key_rows, key_rows.T)
    system = jnp.eye(size_c, dtype=jnp.float32) + jnp.where(
        row_ids > col_ids, beta_rates[:, None] * decays * key_gram, 0.0
    )
    return (cum_log, growth, decays, system)


def group_step(carried, pieces):
    queries, key_rows, values, beta_rates, gate_log = pieces
    head_dim = key_rows.shape[1]
    cum_log, growth, decays, system = group_terms(key_rows, beta_rates, gate_log)
    right_side = beta_rates[:, None] * jnp.concatenate([values, growth[:, None] * key_rows], axis=1)
    solved = lax.linalg.triangular_solve(
        system, right_side, left_side=True, lower=True, unit_diagonal=True
    )
    upd_vals = solved[:, :head_dim]
    wy_keys = solved[:, head_dim:]
    fresh_vals = upd_vals - exact_dot(wy_keys, carried.T)
    outputs = growth[:, None] * exact_dot(queries, carried.T) + exact_dot(
        exact_dot(queries, key_rows.T) * decays, fresh_vals
    )
    tail_decay = jnp.exp(cum_log[-1] - cum_log)
    carried = growth[-1] * carried + exact_dot((fresh_vals * tail_decay[:, None]).T, key_rows)
    return (carried, outputs)


def into_groups(array):
    count = array.shape[0] // GROUP
    return array.reshape((count, GROUP) + array.shape[1:])


def head_forward(queries, key_rows, values, beta_rates, gate_log, carried):
    carried, outputs = lax.scan(
        group_step,
        carried,
        (
            into_groups(queries),
            into_groups(key_rows),
            into_groups(values),
            into_groups(beta_rates),
            into_groups(gate_log),
        ),
    )
    return (outputs.reshape(queries.shape), carried)


def block_forward(queries, key_rows, values, beta_rates, gate_log, carried):
    token_count, width = queries.shape
    head_count = carried.shape[0]

    def split_heads(array):
        return array.reshape(token_count, head_count, HD).transpose(1, 0, 2)

    outputs, carried = jax.vmap(head_forward)(
        split_heads(queries),
        split_heads(key_rows),
        split_heads(values),
        beta_rates,
        gate_log,
        carried,
    )
    return (outputs.transpose(1, 0, 2).reshape(token_count, width), carried)


def transit_step(product, pieces):
    key_rows, beta_rates, gate_log = pieces
    head_dim = key_rows.shape[1]
    cum_log, growth, decays, system = group_terms(key_rows, beta_rates, gate_log)
    right_side = beta_rates[:, None] * growth[:, None] * key_rows
    wy_keys = lax.linalg.triangular_solve(
        system, right_side, left_side=True, lower=True, unit_diagonal=True
    )
    tail_decay = jnp.exp(cum_log[-1] - cum_log)
    group_map = growth[-1] * jnp.eye(head_dim, dtype=jnp.float32) - exact_dot(
        wy_keys.T, tail_decay[:, None] * key_rows
    )
    return (exact_dot(product, group_map), None)


def head_transition(key_rows, beta_rates, gate_log):
    start_map = jnp.eye(key_rows.shape[1], dtype=jnp.float32)
    product, _ = lax.scan(
        transit_step,
        start_map,
        (into_groups(key_rows), into_groups(beta_rates), into_groups(gate_log)),
    )
    return product


def window_backward(queries, key_rows, values, dout, query_pos, key_pos, doc_len):
    q_count, width = queries.shape
    k_count = key_rows.shape[0]
    heads_here = width // HD
    scale = 1.0 / math.sqrt(HD)
    q_heads = queries.reshape(q_count, heads_here, HD)
    k_heads = key_rows.reshape(k_count, heads_here, HD)
    v_heads = values.reshape(k_count, heads_here, HD)
    d_heads = dout.reshape(q_count, heads_here, HD)
    scores = (
        jnp.einsum("qhd,khd->hqk", q_heads, k_heads, preferred_element_type=jnp.float32) * scale
    )
    doc_start = query_pos // doc_len * doc_len
    visible = (
        (key_pos[None, :] <= query_pos[:, None])
        & (key_pos[None, :] > query_pos[:, None] - WINDOW)
        & (key_pos[None, :] >= doc_start[:, None])
    )
    scores = jnp.where(visible[None], scores, -jnp.inf)
    row_max = jnp.max(scores, axis=2, keepdims=True)
    expo = jnp.exp(scores - row_max)
    weights = expo / jnp.sum(expo, axis=2, keepdims=True)
    weights_bf = weights.astype(jnp.bfloat16)
    dweights = jnp.einsum("qhd,khd->hqk", d_heads, v_heads, preferred_element_type=jnp.float32)
    row_dots = jnp.sum(weights * dweights, axis=2, keepdims=True)
    dscore_bf = (weights * (dweights - row_dots)).astype(jnp.bfloat16)
    grad_q = (
        jnp.einsum("hqk,khd->qhd", dscore_bf, k_heads, preferred_element_type=jnp.float32) * scale
    )
    grad_k = (
        jnp.einsum("hqk,qhd->khd", dscore_bf, q_heads, preferred_element_type=jnp.float32) * scale
    )
    grad_v = jnp.einsum("hqk,qhd->khd", weights_bf, d_heads, preferred_element_type=jnp.float32)
    return (
        grad_q.reshape(q_count, width),
        grad_k.reshape(k_count, width),
        grad_v.reshape(k_count, width),
    )


def shards(
    att_q,
    att_k,
    att_v,
    att_dy,
    att_out_w,
    gdn_q,
    gdn_k,
    gdn_v,
    gdn_beta,
    gdn_gate,
    gdn_state,
    gdn_dy,
    gdn_out_w,
):
    tok_rows, width = att_q.shape
    seq_count = lax.axis_size("seq")
    dev_index = lax.axis_index("seq")
    reach = WINDOW // tok_rows
    doc_len = tok_rows * seq_count // DOCS
    per_doc = seq_count // DOCS
    att_add = jnp.einsum(
        "tn,hn->th",
        lax.all_gather(att_dy, "head", axis=1, tiled=True),
        att_out_w,
        preferred_element_type=jnp.float32,
    )
    gdn_add = jnp.einsum(
        "tn,hn->th",
        lax.all_gather(gdn_dy, "head", axis=1, tiled=True),
        gdn_out_w,
        preferred_element_type=jnp.float32,
    )
    att_dout = att_add.astype(jnp.bfloat16)
    gdn_dout = gdn_add.astype(jnp.bfloat16)
    own_pair = jnp.stack([att_k, att_v])
    key_blocks = []
    for shift_by in range(reach, 0, -1):
        key_blocks.append(passed_along(own_pair, "seq", shift_by))
    key_blocks.append(own_pair)
    joined = jnp.concatenate(key_blocks, axis=1)
    query_pos = dev_index * tok_rows + jnp.arange(tok_rows, dtype=jnp.int32)
    key_pos = (dev_index - reach) * tok_rows + jnp.arange((reach + 1) * tok_rows, dtype=jnp.int32)
    grad_q, grad_k, grad_v = window_backward(
        att_q, joined[0], joined[1], att_dout, query_pos, key_pos, doc_len
    )
    total_k = grad_k[reach * tok_rows :]
    total_v = grad_v[reach * tok_rows :]
    for shift_by in range(1, reach + 1):
        low_row = (reach - shift_by) * tok_rows
        returned = passed_along(
            jnp.stack([grad_k[low_row : low_row + tok_rows], grad_v[low_row : low_row + tok_rows]]),
            "seq",
            -shift_by,
        )
        total_k = total_k + returned[0]
        total_v = total_v + returned[1]
    att_dq = grad_q.astype(jnp.bfloat16)
    att_dk = total_k.astype(jnp.bfloat16)
    att_dv = total_v.astype(jnp.bfloat16)
    q_float = gdn_q.astype(jnp.float32)
    k_float = gdn_k.astype(jnp.float32)
    v_float = gdn_v.astype(jnp.float32)
    start_state = gdn_state[0]
    heads_here = start_state.shape[0]
    (outputs, final_state), pull_back = jax.vjp(
        block_forward, q_float, k_float, v_float, gdn_beta, gdn_gate, start_state
    )
    first_pass = pull_back((gdn_dout.astype(jnp.float32), jnp.zeros_like(final_state)))
    local_term = first_pass[5]
    head_keys = k_float.reshape(tok_rows, heads_here, HD).transpose(1, 0, 2)
    transit = jax.vmap(head_transition)(head_keys, gdn_beta, gdn_gate)
    keep_mask = (dev_index % per_doc != 0).astype(jnp.float32)

    def link_step(step_id, adjoint):
        start_term = keep_mask * (
            jnp.einsum("hab,hcb->hac", adjoint, transit, precision=lax.Precision.HIGHEST)
            + local_term
        )
        return passed_along(start_term, "seq", -1)

    adjoint_end = lax.fori_loop(0, per_doc - 1, link_step, jnp.zeros_like(local_term))
    second_pass = pull_back((jnp.zeros_like(outputs), adjoint_end))
    gdn_dq = (first_pass[0] + second_pass[0]).astype(jnp.bfloat16)
    gdn_dk = (first_pass[1] + second_pass[1]).astype(jnp.bfloat16)
    gdn_dv = (first_pass[2] + second_pass[2]).astype(jnp.bfloat16)
    gdn_dbeta = first_pass[3] + second_pass[3]
    gdn_dgate = first_pass[4] + second_pass[4]
    return (att_dq, att_dk, att_dv, gdn_dq, gdn_dk, gdn_dv, gdn_dbeta, gdn_dgate)


def solution(mesh):
    return jax.shard_map(
        shards,
        mesh=mesh,
        in_specs=(
            P("seq", "head"),
            P("seq", "head"),
            P("seq", "head"),
            P("seq", "head"),
            P("head", None),
            P("seq", "head"),
            P("seq", "head"),
            P("seq", "head"),
            P("head", "seq"),
            P("head", "seq"),
            P("seq", "head", None, None),
            P("seq", "head"),
            P("head", None),
        ),
        out_specs=(
            P("seq", "head"),
            P("seq", "head"),
            P("seq", "head"),
            P("seq", "head"),
            P("seq", "head"),
            P("seq", "head"),
            P("head", "seq"),
            P("head", "seq"),
        ),
        check_vma=False,
    )
```

profile of v0, /device:TPU:6, one launch (start us, length us, event | category | flops | bytes accessed | tf_op | source)
XLA Modules:
  0.0 1060.7 jit_solution(11453961267288795197)
XLA Ops:
  3.7 9.1 collective-permute-start.1
  35.4 98.9 %while.140 = (s32[]{:T(128)}, f32[4,128,128]{2,1,0:T(8,128)S(1)}, f32[2,4,64]{2,1,0:T(4,128)}, f32[2,4,64,64]{3,2,1,0:T(8,128)}, f32[2,4,64,64]{3,2,1,0:T(8,128)...) while((s32[]{:T(128)}, f32[4,128,128]{2,1,0:T(8,128)S(1)}, ...), condition=%wide.region_5.6_spmd.clone.clone, body=%wide.region_3.5_spmd.clone.clone.sunk | while | flops 252564032 | bytes 14042361 | solution.py:65
  41.4 20.3 %custom-call.54 = f32[4,1,64,64]{2,3,1,0:T(8,128)} custom-call(f32[4,1,64,64]{3,2,1,0:T(8,128)S(1)} %get-tuple-element.3993), custom_call_target="InvertDiagBlocksLowerTriangular" | custom-call | tf_op jit(solution)/shard_map/jvp(vmap())/while/body/eval_jaxpr/triangular_solve | solution.py:45
  90.9 20.3 %custom-call.54 = f32[4,1,64,64]{2,3,1,0:T(8,128)} custom-call(f32[4,1,64,64]{3,2,1,0:T(8,128)S(1)} %get-tuple-element.3993), custom_call_target="InvertDiagBlocksLowerTriangular" | custom-call | tf_op jit(solution)/shard_map/jvp(vmap())/while/body/eval_jaxpr/triangular_solve | solution.py:45
  135.7 13.8 %all_gather.7 = bf16[128,2048]{1,0:T(8,128)(2,1)S(1)} all-gather(bf16[128,512]{1,0:T(8,128)(2,1)} %param.38), channel_id=1, replica_groups=mesh['seq'=64,'head'=4] {'head'}, dimensions={1}, use_global_device_ids=true | all-gather | bytes 655360 | tf_op jit(solution)/shard_map/all_gather | solution.py:191
  154.4 111.5 %while.141 = (s32[]{:T(128)}, f32[4,128,128]{2,1,0:T(8,128)S(1)}, f32[2,4,64,128]{3,2,0,1:T(8,128)}, f32[2,4,64,128]{3,2,0,1:T(8,128)}, f32[2,4,64,128]{3,2,0,1:...) while((s32[]{:T(128)}, f32[4,128,128]{2,1,0:T(8,128)S(1)}, ...), condition=%wide.region_17.20_spmd.clone, body=%wide.region_6.19_spmd.clone.sunk | while | flops 568096064 | bytes 26133992 | solution.py:65
  161.7 20.4 %custom-call.55 = f32[4,1,64,64]{2,3,1,0:T(8,128)S(1)} custom-call(f32[4,1,64,64]{3,2,1,0:T(8,128)} %fusion.524), custom_call_target="InvertDiagBlocksLowerTriangular" | custom-call | tf_op jit(solution)/shard_map/transpose(jvp(vmap()))/while/body/eval_jaxpr/triangular_solve/custom-call.0 | solution.py:45
  217.5 20.4 %custom-call.55 = f32[4,1,64,64]{2,3,1,0:T(8,128)S(1)} custom-call(f32[4,1,64,64]{3,2,1,0:T(8,128)} %fusion.524), custom_call_target="InvertDiagBlocksLowerTriangular" | custom-call | tf_op jit(solution)/shard_map/transpose(jvp(vmap()))/while/body/eval_jaxpr/triangular_solve/custom-call.0 | solution.py:45
  267.5 51.2 %while.137 = (s32[]{:T(128)}, f32[4,128,128]{1,2,0:T(8,128)}, f32[2,4,64]{2,1,0:T(4,128)}, f32[2,4,64]{2,1,0:T(4,128)}, f32[2,4,64,128]{3,2,1,0:T(8,128)S(1)}, /*index=5*/s32[]{:T(128)}, f32[]{:T(128)}) while((s32[]{:T(128)}, f32[4,128,128]{1,2,0:T(8,128)}, f32[2,4,64]{2,1,0:T(4,128)}, f32[2,4,64]{2,1,0:T(4,128)}, ...), condition=%wide.region_20.23_spmd, body=%wide.region_18.22_spmd.sunk | while | flops 201748800 | bytes 2712757 | solution.py:114
  269.9 19.7 %custom-call.52 = f32[4,1,64,64]{2,3,1,0:T(8,128)S(1)} custom-call(f32[4,1,64,64]{3,2,1,0:T(8,128)S(1)} %fusion.442), custom_call_target="InvertDiagBlocksLowerTriangular" | custom-call | tf_op jit(solution)/shard_map/vmap()/while/body/eval_jaxpr/triangular_solve | solution.py:102
  295.5 19.7 %custom-call.52 = f32[4,1,64,64]{2,3,1,0:T(8,128)S(1)} custom-call(f32[4,1,64,64]{3,2,1,0:T(8,128)S(1)} %fusion.442), custom_call_target="InvertDiagBlocksLowerTriangular" | custom-call | tf_op jit(solution)/shard_map/vmap()/while/body/eval_jaxpr/triangular_solve | solution.py:102
  320.6 380.0 %while.138 = (s32[]{:T(128)}, f32[4,128,128]{2,1,0:T(8,128)S(1)}, f32[]{:T(128)}, f32[4,128,128]{2,1,0:T(8,128)}, f32[4,128,128]{2,1,0:T(8,128)S(1)}, /*index=5*/s32[]{:T(128)}) while((s32[]{:T(128)}, f32[4,128,128]{2,1,0:T(8,128)S(1)}, f32[]{:T(128)}, f32[4,128,128]{2,1,0:T(8,128)}, f32[4,128,128]{2,1,0:T(8,128)S(1)}, ...), condition=%wide.region_22.25_spmd, body=%wide.region_21.24_spmd.sunk | while | flops 100794368 | bytes 2097265 | solution.py:243
  332.8 5.8 collective-permute-start
  345.1 5.8 collective-permute-start
  369.8 5.8 collective-permute-start
  706.0 110.3 %while.139 = (s32[]{:T(128)}, f32[4,128,128]{2,1,0:T(8,128)S(1)}, f32[2,4,64,128]{3,2,0,1:T(8,128)}, f32[2,4,64,128]{3,2,0,1:T(8,128)}, f32[2,4,64,128]{3,2,0,1:...) while((s32[]{:T(128)}, f32[4,128,128]{2,1,0:T(8,128)S(1)}, ...), condition=%wide.region_34.37_spmd.clone, body=%wide.region_23.36_spmd.clone.sunk | while | flops 567768640 | bytes 22979488 | solution.py:65
  713.3 20.4 %custom-call.53 = f32[4,1,64,64]{2,3,1,0:T(8,128)S(1)} custom-call(f32[4,1,64,64]{3,2,1,0:T(8,128)} %fusion.475), custom_call_target="InvertDiagBlocksLowerTriangular" | custom-call | tf_op jit(solution)/shard_map/transpose(jvp(vmap()))/while/body/eval_jaxpr/triangular_solve/custom-call.0 | solution.py:45
  768.4 20.4 %custom-call.53 = f32[4,1,64,64]{2,3,1,0:T(8,128)S(1)} custom-call(f32[4,1,64,64]{3,2,1,0:T(8,128)} %fusion.475), custom_call_target="InvertDiagBlocksLowerTriangular" | custom-call | tf_op jit(solution)/shard_map/transpose(jvp(vmap()))/while/body/eval_jaxpr/triangular_solve/custom-call.0 | solution.py:45
  816.4 13.0 %all_gather.6 = bf16[128,2048]{1,0:T(8,128)(2,1)S(1)} all-gather(bf16[128,512]{1,0:T(8,128)(2,1)} %param.30), channel_id=1, replica_groups=mesh['seq'=64,'head'=4] {'head'}, dimensions={1}, use_global_device_ids=true | all-gather | bytes 655360 | tf_op jit(solution)/shard_map/all_gather | solution.py:185
  915.6 12.3 %collective-permute-start.14 = (f32[2,128,512]{1,2,0:T(8,128)}, f32[2,128,512]{1,2,0:T(8,128)}, u32[]{:S(2)}, u32[]{:S(2)}) collective-permute-start(f32[2,128,512]{1,2,0:T(8,128)} %pad_maximum_fusion.7), channel_id=1, source_target_pairs={{24,0},{28,4},{32,8},{36,12},{40,16},{44,20},{48,24},{52,28},{56,3... | collective-permute-start | bytes 1572872 | tf_op jit(solution)/shard_map/ppermute | solution.py:17
  930.4 7.6 collective-permute-start.16
  947.9 32.9 %collective-permute-done.12 = f32[2,128,512]{1,2,0:T(8,128)} collective-permute-done((f32[2,128,512]{1,2,0:T(8,128)}, f32[2,128,512]{1,2,0:T(8,128)}, u32[]{:S(2)}, u32[]{:S(2)}) %collective-permute-start.12) | collective-permute-done | bytes 524320 | tf_op jit(solution)/shard_map/ppermute | solution.py:17
  980.8 21.3 %collective-permute-done.13 = f32[2,128,512]{1,2,0:T(8,128)} collective-permute-done((f32[2,128,512]{1,2,0:T(8,128)}, f32[2,128,512]{1,2,0:T(8,128)}, u32[]{:S(2)}, u32[]{:S(2)}) %collective-permute-start.13) | collective-permute-done | bytes 524320 | tf_op jit(solution)/shard_map/ppermute | solution.py:17
  1002.1 54.7 %collective-permute-done.14 = f32[2,128,512]{1,2,0:T(8,128)} collective-permute-done((f32[2,128,512]{1,2,0:T(8,128)}, f32[2,128,512]{1,2,0:T(8,128)}, u32[]{:S(2)}, u32[]{:S(2)}) %collective-permute-start.14) | collective-permute-done | bytes 524320 | tf_op jit(solution)/shard_map/ppermute | solution.py:17
  (660 shorter events, 713.9 us)
Async XLA Ops:
  3.7 834.7 %collective-permute-start.1 = (bf16[2,128,512]{1,2,0:T(8,128)(2,1)}, bf16[2,128,512]{1,2,0:T(8,128)(2,1)}, u32[]{:S(2)}, u32[]{:S(2)}) collective-permute-start(bf16[2,128,512]{1,2,0:T(8,128)(2,1)} %pad_maximum_fusion.10), channel_id=1, source_target_pairs={{0,32},{4,36},{8,40},{12,44},{16,48},{20,52},{24,56},{28,60},{32,6... | collective-permute-start | bytes 786440 | tf_op jit(solution)/shard_map/ppermute | solution.py:17
  12.8 828.6 %collective-permute-start.2 = (bf16[2,128,512]{1,2,0:T(8,128)(2,1)}, bf16[2,128,512]{1,2,0:T(8,128)(2,1)}, u32[]{:S(2)}, u32[]{:S(2)}) collective-permute-start(bf16[2,128,512]{1,2,0:T(8,128)(2,1)} %pad_maximum_fusion.10), channel_id=1, source_target_pairs={{0,28},{4,32},{8,36},{12,40},{16,44},{20,48},{24,52},{28,56},{32,6... | collective-permute-start | bytes 786440 | tf_op jit(solution)/shard_map/ppermute | solution.py:17
  15.8 828.5 %collective-permute-start.3 = (bf16[2,128,512]{1,2,0:T(8,128)(2,1)}, bf16[2,128,512]{1,2,0:T(8,128)(2,1)}, u32[]{:S(2)}, u32[]{:S(2)}) collective-permute-start(bf16[2,128,512]{1,2,0:T(8,128)(2,1)} %pad_maximum_fusion.10), channel_id=1, source_target_pairs={{0,24},{4,28},{8,32},{12,36},{16,40},{20,44},{24,48},{28,52},{32,5... | collective-permute-start | bytes 786440 | tf_op jit(solution)/shard_map/ppermute | solution.py:17
  18.5 829.0 %collective-permute-start.4 = (bf16[2,128,512]{1,2,0:T(8,128)(2,1)}, bf16[2,128,512]{1,2,0:T(8,128)(2,1)}, u32[]{:S(2)}, u32[]{:S(2)}) collective-permute-start(bf16[2,128,512]{1,2,0:T(8,128)(2,1)} %pad_maximum_fusion.10), channel_id=1, source_target_pairs={{0,20},{4,24},{8,28},{12,32},{16,36},{20,40},{24,44},{28,48},{32,5... | collective-permute-start | bytes 786440 | tf_op jit(solution)/shard_map/ppermute | solution.py:17
  332.8 10.0 collective-permute-start
  345.1 10.0 collective-permute-start
  369.8 10.0 collective-permute-start
  443.8 10.0 collective-permute-start
  456.1 10.0 collective-permute-start
  468.5 10.0 collective-permute-start
  480.8 10.0 collective-permute-start
  554.8 10.0 collective-permute-start
  700.5 148.0 %collective-permute-start.5 = (bf16[2,128,512]{1,2,0:T(8,128)(2,1)}, bf16[2,128,512]{1,2,0:T(8,128)(2,1)}, u32[]{:S(2)}, u32[]{:S(2)}) collective-permute-start(bf16[2,128,512]{1,2,0:T(8,128)(2,1)} %pad_maximum_fusion.10), channel_id=1, source_target_pairs={{0,16},{4,20},{8,24},{12,28},{16,32},{20,36},{24,40},{28,44},{32,4... | collective-permute-start | bytes 786440 | tf_op jit(solution)/shard_map/ppermute | solution.py:17
  838.4 15.2 %collective-permute-start.6 = (bf16[2,128,512]{1,2,0:T(8,128)(2,1)}, bf16[2,128,512]{1,2,0:T(8,128)(2,1)S(1)}, u32[]{:S(2)}, u32[]{:S(2)}) collective-permute-start(bf16[2,128,512]{1,2,0:T(8,128)(2,1)} %pad_maximum_fusion.10), channel_id=1, source_target_pairs={{0,12},{4,16},{8,20},{12,24},{16,28},{20,32},{24,36},{28,40},{32,4... | collective-permute-start | bytes 786440 | tf_op jit(solution)/shard_map/ppermute | solution.py:17
  841.3 14.4 %collective-permute-start.7 = (bf16[2,128,512]{1,2,0:T(8,128)(2,1)}, bf16[2,128,512]{1,2,0:T(8,128)(2,1)S(1)}, u32[]{:S(2)}, u32[]{:S(2)}) collective-permute-start(bf16[2,128,512]{1,2,0:T(8,128)(2,1)} %pad_maximum_fusion.10), channel_id=1, source_target_pairs={{0,8},{4,12},{8,16},{12,20},{16,24},{20,28},{24,32},{28,36},{32,40... | collective-permute-start | bytes 786440 | tf_op jit(solution)/shard_map/ppermute | solution.py:17
  844.3 12.7 %collective-permute-start.8 = (bf16[2,128,512]{1,2,0:T(8,128)(2,1)}, bf16[2,128,512]{1,2,0:T(8,128)(2,1)S(1)}, u32[]{:S(2)}, u32[]{:S(2)}) collective-permute-start(bf16[2,128,512]{1,2,0:T(8,128)(2,1)} %pad_maximum_fusion.10), channel_id=1, source_target_pairs={{0,4},{4,8},{8,12},{12,16},{16,20},{20,24},{24,28},{28,32},{32,36}... | collective-permute-start | bytes 786440 | tf_op jit(solution)/shard_map/ppermute | solution.py:17
  874.6 41.0 %collective-permute-start.9 = (f32[2,128,512]{1,2,0:T(8,128)}, f32[2,128,512]{1,2,0:T(8,128)}, u32[]{:S(2)}, u32[]{:S(2)}) collective-permute-start(f32[2,128,512]{1,2,0:T(8,128)} %pad_maximum_fusion.2), channel_id=1, source_target_pairs={{4,0},{8,4},{12,8},{16,12},{20,16},{24,20},{28,24},{32,28},{36,32}... | collective-permute-start | bytes 1572872 | tf_op jit(solution)/shard_map/ppermute | solution.py:17
  882.8 45.1 %collective-permute-start.10 = (f32[2,128,512]{1,2,0:T(8,128)}, f32[2,128,512]{1,2,0:T(8,128)}, u32[]{:S(2)}, u32[]{:S(2)}) collective-permute-start(f32[2,128,512]{1,2,0:T(8,128)} %pad_maximum_fusion.3), channel_id=1, source_target_pairs={{8,0},{12,4},{16,8},{20,12},{24,16},{28,20},{32,24},{36,28},{40,32... | collective-permute-start | bytes 1572872 | tf_op jit(solution)/shard_map/ppermute | solution.py:17
  891.4 39.0 %collective-permute-start.11 = (f32[2,128,512]{1,2,0:T(8,128)}, f32[2,128,512]{1,2,0:T(8,128)}, u32[]{:S(2)}, u32[]{:S(2)}) collective-permute-start(f32[2,128,512]{1,2,0:T(8,128)} %pad_maximum_fusion.4), channel_id=1, source_target_pairs={{12,0},{16,4},{20,8},{24,12},{28,16},{32,20},{36,24},{40,28},{44,3... | collective-permute-start | bytes 1572872 | tf_op jit(solution)/shard_map/ppermute | solution.py:17
  897.0 83.8 %collective-permute-start.12 = (f32[2,128,512]{1,2,0:T(8,128)}, f32[2,128,512]{1,2,0:T(8,128)}, u32[]{:S(2)}, u32[]{:S(2)}) collective-permute-start(f32[2,128,512]{1,2,0:T(8,128)} %pad_maximum_fusion.5), channel_id=1, source_target_pairs={{16,0},{20,4},{24,8},{28,12},{32,16},{36,20},{40,24},{44,28},{48,3... | collective-permute-start | bytes 1572872 | tf_op jit(solution)/shard_map/ppermute | solution.py:17
  902.7 99.4 %collective-permute-start.13 = (f32[2,128,512]{1,2,0:T(8,128)}, f32[2,128,512]{1,2,0:T(8,128)}, u32[]{:S(2)}, u32[]{:S(2)}) collective-permute-start(f32[2,128,512]{1,2,0:T(8,128)} %pad_maximum_fusion.6), channel_id=1, source_target_pairs={{20,0},{24,4},{28,8},{32,12},{36,16},{40,20},{44,24},{48,28},{52,3... | collective-permute-start | bytes 1572872 | tf_op jit(solution)/shard_map/ppermute | solution.py:17
  915.6 141.1 %collective-permute-start.14 = (f32[2,128,512]{1,2,0:T(8,128)}, f32[2,128,512]{1,2,0:T(8,128)}, u32[]{:S(2)}, u32[]{:S(2)}) collective-permute-start(f32[2,128,512]{1,2,0:T(8,128)} %pad_maximum_fusion.7), channel_id=1, source_target_pairs={{24,0},{28,4},{32,8},{36,12},{40,16},{44,20},{48,24},{52,28},{56,3... | collective-permute-start | bytes 1572872 | tf_op jit(solution)/shard_map/ppermute | solution.py:17
  928.0 128.8 %collective-permute-start.15 = (f32[2,128,512]{1,2,0:T(8,128)}, f32[2,128,512]{1,2,0:T(8,128)}, u32[]{:S(2)}, u32[]{:S(2)}) collective-permute-start(f32[2,128,512]{1,2,0:T(8,128)} %pad_maximum_fusion.8), channel_id=1, source_target_pairs={{28,0},{32,4},{36,8},{40,12},{44,16},{48,20},{52,24},{56,28},{60,3... | collective-permute-start | bytes 1572872 | tf_op jit(solution)/shard_map/ppermute | solution.py:17
  930.4 126.3 %collective-permute-start.16 = (f32[2,128,512]{1,2,0:T(8,128)}, f32[2,128,512]{1,2,0:T(8,128)}, u32[]{:S(2)}, u32[]{:S(2)}) collective-permute-start(f32[2,128,512]{1,2,0:T(8,128)} %pad_maximum_fusion.9), channel_id=1, source_target_pairs={{32,0},{36,4},{40,8},{44,12},{48,16},{52,20},{56,24},{60,28},{64,3... | collective-permute-start | bytes 1572872 | tf_op jit(solution)/shard_map/ppermute | solution.py:17
  (122 other events, 1174.9 us)
where the time goes:
time: 1080 us; the launch traced here: 1060 us
  other arithmetic  248 us (23%)
  waiting for transfers between devices  246 us (23%)
  starting transfers between devices  240 us (22%)
  matrix products  185 us (17%)
  local copies, waits for them, and re-layouts  112 us (10%)
  blocking collectives  26.8 us (2%)
    ppermute x47, waiting for transfers between devices, passed_along(): lax.ppermute(value, axis, [(source, source + steps) for source in range(i...  246 us
    ppermute x47, starting transfers between devices, passed_along(): lax.ppermute(value, axis, [(source, source + steps) for source in range(i...  240 us
    another operation x28, other arithmetic, group_step(): lax.linalg.triangular_solve(system, right_side, left_side=True, lower=Tru...  129 us
    dot_general x64, matrix products, exact_dot(): return jnp.dot(left, right, precision=lax.Precision.HIGHEST)  74 us
    dot_general x31, matrix products, link_step(): jnp.einsum('hab,hcb->hac', adjoint, transit, precision=lax.Precision.HIGH...  72.5 us
    another operation x8, other arithmetic, transit_step(): lax.linalg.triangular_solve(system, right_side, left_side=True, lower=Tru...  39.5 us
  transfers between devices with their start and end apart: 47, of which 37 were waited for; matrix products, arithmetic and copies ran while one was open for 48% of the time, Pallas kernels for 0%

commit v1 on v0

v1 whole, which is shorter than its diff:
```python
import math

import jax
import jax.numpy as jnp
from jax import lax
from jax.experimental import pallas as pl
from jax.experimental.pallas import tpu as pltpu
from jax.sharding import PartitionSpec as P

HD = 128
PAIR = 256
RING = 4
SEG = 4
SEGS = 8
DOCS = 2
F32 = jnp.float32
BF16 = jnp.bfloat16
NN = (((1,), (0,)), ((), ()))
NT = (((1,), (1,)), ((), ()))
TN = (((0,), (0,)), ((), ()))
FAR = -1e30


def dot(left, right, dims):
    return lax.dot_general(left, right, dims, preferred_element_type=F32)


def exact(left, right, dims):
    return lax.dot_general(
        left, right, dims, precision=lax.Precision.HIGHEST, preferred_element_type=F32
    )


def split(value):
    high = value.astype(BF16)
    return high, (value - high.astype(F32)).astype(BF16)


def dot_l(left, right, dims):
    high, low = split(left)
    return dot(high, right, dims) + dot(low, right, dims)


def dot_r(left, right, dims):
    high, low = split(right)
    return dot(left, high, dims) + dot(left, low, dims)


def dot3(left, right, dims):
    lh, ll = split(left)
    rh, rl = split(right)
    return dot(lh, rh, dims) + (dot(lh, rl, dims) + dot(ll, rh, dims))


def grid_ids(rows, cols):
    return (
        lax.broadcasted_iota(jnp.int32, (rows, cols), 0),
        lax.broadcasted_iota(jnp.int32, (rows, cols), 1),
    )


def head_cols(head):
    return slice(head * HD, (head + 1) * HD)


def token_rates(beta, gate, heads):
    rows, cols = grid_ids(HD, HD)
    pad = jnp.zeros((8 - heads, HD), F32)
    beta8 = jnp.concatenate([beta, pad])
    gate8 = jnp.concatenate([gate, pad])
    upto = (rows <= cols).astype(F32)
    crow = exact(gate8, upto, NN)
    ccol = exact((cols <= rows).astype(F32), gate8, NT)
    bcol = exact((cols == rows).astype(F32), beta8, NT)
    return crow, ccol, bcol, beta8


def gdn_pre_body(q_ref, k_ref, beta_ref, gate_ref, m_ref, n_ref, delta_ref, *, heads):
    rows, cols = grid_ids(HD, HD)
    crow, ccol, bcol, brow = token_rates(beta_ref[...], gate_ref[...], heads)
    lower = rows >= cols
    strict = rows > cols
    eye = (rows == cols).astype(F32)
    systems = []
    mixes = []
    for h in range(heads):
        k = k_ref[:, head_cols(h)]
        q = q_ref[:, head_cols(h)]
        decay = jnp.exp(jnp.minimum(ccol[:, h : h + 1] - crow[h : h + 1, :], 0.0))
        systems.append(jnp.where(strict, bcol[:, h : h + 1] * decay * dot(k, k, NT), 0.0))
        mixes.append(jnp.where(lower, decay * dot(q, k, NT), 0.0))
    pair = (rows >> 1) == (cols >> 1)
    inverse = [eye - jnp.where(pair, s, 0.0) for s in systems]
    for level in range(1, 7):
        ring = ((rows >> (level + 1)) == (cols >> (level + 1))) & ((rows >> level) != (cols >> level))
        part = [dot3(m, jnp.where(ring, s, 0.0), NN) for m, s in zip(inverse, systems)]
        inverse = [m - dot3(x, m, NN) for m, x in zip(inverse, part)]
    for h in range(heads):
        k = k_ref[:, head_cols(h)]
        q = q_ref[:, head_cols(h)]
        last = crow[h : h + 1, HD - 1 :]
        grow = jnp.exp(crow[h : h + 1, :])
        gcol = jnp.exp(ccol[:, h : h + 1])
        tcol = jnp.exp(jnp.minimum(last - ccol[:, h : h + 1], 0.0))
        wy = dot_l(inverse[h] * (brow[h : h + 1, :] * grow), k, NN)
        m_ref[h] = inverse[h]
        n_ref[h] = gcol * q.astype(F32) - dot3(mixes[h], wy, NN)
        delta_ref[h, :HD, :] = dot_r(k, tcol * wy, TN).astype(BF16)
        total = jnp.broadcast_to(jnp.exp(last), (16, HD))
        high = total.astype(BF16).astype(F32)
        mid = (total - high).astype(BF16).astype(F32)
        low = total - high - mid
        tile_row = lax.broadcasted_iota(jnp.int32, (16, HD), 0)
        tile = jnp.where(
            tile_row == 0, high, jnp.where(tile_row == 1, mid, jnp.where(tile_row == 2, low, 0.0))
        )
        delta_ref[h, HD:, :] = tile.astype(BF16)


def project(parts, w_ref, owners, width):
    total = None
    for part, owner in zip(parts, owners):
        span = pl.ds(pl.multiple_of(owner * width, width), width)
        term = dot(part[...], w_ref[:, span], NT)
        total = term if total is None else total + term
    return total.astype(BF16)


def shard_owners():
    own = lax.axis_index("head")
    count = lax.axis_size("head")
    return [(own - shift + count) % count for shift in range(count)]


def gdn_dout_body(d0, d1, d2, d3, w_ref, n_ref, delta_ref, dout_ref, send_ref, *, heads):
    dout = project((d0, d1, d2, d3), w_ref, shard_owners(), d0.shape[1])
    dout_ref[...] = dout
    for h in range(heads):
        send_ref[h, : HD + 16, :] = delta_ref[h]
        send_ref[h, HD + 16 :, :] = dot_r(dout[:, head_cols(h)], n_ref[h], TN).astype(BF16)


def unpack_map(payload):
    delta = payload[:HD]
    tile = payload[HD : HD + 16].astype(F32)
    gain = tile[0:1] + tile[1:2] + tile[2:3]
    return gain, delta, payload[HD + 16 :].astype(F32)


def chain_fold_body(blocks_ref, out_ref):
    gain, delta, local = unpack_map(blocks_ref[SEG - 1])
    both = jnp.concatenate([delta.astype(F32), local])
    for b in range(SEG - 2, -1, -1):
        next_gain, next_delta, next_local = unpack_map(blocks_ref[b])
        moved = next_gain * both - dot_l(both, next_delta, NN)
        both = moved + jnp.concatenate([gain * next_delta.astype(F32), next_local])
        gain = gain * next_gain
    out_ref[:HD, :] = both[:HD].astype(BF16)
    out_ref[HD + 16 :, :] = both[HD:].astype(BF16)
    total = jnp.broadcast_to(gain, (16, HD))
    high = total.astype(BF16).astype(F32)
    mid = (total - high).astype(BF16).astype(F32)
    low = total - high - mid
    tile_row = lax.broadcasted_iota(jnp.int32, (16, HD), 0)
    tile = jnp.where(
        tile_row == 0, high, jnp.where(tile_row == 1, mid, jnp.where(tile_row == 2, low, 0.0))
    )
    out_ref[HD : HD + 16, :] = tile.astype(BF16)


def chain_walk_body(*refs):
    later, blocks_ref, out_ref = refs[: SEGS - 1], refs[SEGS - 1], refs[SEGS]
    adjoint = jnp.zeros((HD, HD), F32)

    def step(adjoint, payload):
        gain, delta, local = unpack_map(payload)
        high, low = split(adjoint)
        both = dot(jnp.concatenate([high, low]), delta, NN)
        return gain * adjoint - (both[:HD] + both[HD:]) + local

    for seg in range(SEGS - 2, -1, -1):
        adjoint = step(adjoint, later[seg][...])
    for b in range(SEG - 1, -1, -1):
        out_ref[b] = adjoint.astype(BF16)
        if b:
            adjoint = step(adjoint, blocks_ref[b])


def gdn_post_body(
    q_ref, k_ref, v_ref, beta_ref, gate_ref, s_ref, m_ref, dout_ref, a_ref,
    dq_ref, dk_ref, dv_ref, dbeta_ref, dgate_ref, *, heads,
):
    rows, cols = grid_ids(HD, HD)
    crow, ccol, bcol, _ = token_rates(beta_ref[...], gate_ref[...], heads)
    lower = rows >= cols
    strict = rows > cols
    after = jnp.zeros((HD, HD), F32)
    before = jnp.zeros((HD, HD), F32)
    rates = jnp.zeros((HD, HD), F32)
    row8 = lax.broadcasted_iota(jnp.int32, (8, HD), 0)
    taken = jnp.zeros((8, HD), F32)
    whole = jnp.zeros((8, HD), F32)
    for h in range(heads):
        q = q_ref[:, head_cols(h)]
        k = k_ref[:, head_cols(h)]
        v = v_ref[:, head_cols(h)].astype(F32)
        dout = dout_ref[:, head_cols(h)]
        state = s_ref[h]
        inverse = m_ref[h]
        adjoint = a_ref[h]
        b = bcol[:, h : h + 1]
        c = ccol[:, h : h + 1]
        last = crow[h : h + 1, HD - 1 :]
        g = jnp.exp(c)
        t = jnp.exp(jnp.minimum(last - c, 0.0))
        decay = jnp.where(lower, jnp.exp(jnp.minimum(c - crow[h : h + 1, :], 0.0)), 0.0)
        gram = decay * dot(k, k, NT)
        mix = decay * dot(q, k, NT)
        k_s = dot_r(k, state, NT)
        q_s = dot_r(q, state, NT)
        resid = v - g * k_s
        fresh = dot3(inverse, b * resid, NN)
        k_a = dot(k, adjoint, NT)
        dfresh = dot_l(mix, dout, TN) + t * k_a
        dright = dot3(inverse, dfresh, TN)
        dmix = dot_r(dout, fresh, NT)
        dsys = jnp.where(strict, -dot3(dright, fresh, NT), 0.0)
        x_mix = dmix * decay
        x_sys = dsys * (b * decay)
        dq_ref[:, head_cols(h)] = (g * dot_r(dout, state, NN) + dot_l(x_mix, k, NN)).astype(BF16)
        dk = dot_l(x_mix, q, TN) + dot_l(x_sys, k, NN) + dot_l(x_sys, k, TN)
        dk = dk + dot_l(t * fresh, adjoint, NN) - dot3((b * g) * dright, state, NN)
        dk_ref[:, head_cols(h)] = dk.astype(BF16)
        dv_ref[:, head_cols(h)] = (b * dright).astype(BF16)
        dbeta = jnp.sum(dright * resid + dsys * gram, axis=1, keepdims=True)
        flow = dmix * mix + dsys * (b * gram)
        dgrow = jnp.sum(
            g * (dout.astype(F32) * q_s - b * dright * k_s) + flow, axis=1, keepdims=True
        )
        dtail = jnp.sum(t * fresh * k_a, axis=1, keepdims=True)
        ends = jnp.exp(last) * jnp.sum(
            jnp.sum(adjoint.astype(F32) * state, axis=1, keepdims=True), axis=0, keepdims=True
        )
        after = jnp.where(cols == h, dgrow, after)
        before = jnp.where(cols == h, dtail, before)
        rates = jnp.where(cols == h, dbeta, rates)
        taken = jnp.where(row8 == h, jnp.sum(flow, axis=0, keepdims=True), taken)
        whole = jnp.where(row8 == h, ends, whole)
    not_before = (rows >= cols).astype(F32)
    dgate = exact(after, not_before, TN) + exact(before, (rows < cols).astype(F32), TN)
    dgate = dgate[:8] + whole - exact(taken, not_before, NN)
    dgate_ref[...] = dgate[:heads]
    dbeta_ref[...] = exact(rates, (rows == cols).astype(F32), TN)[:heads]


def core_side():
    return lax.axis_index("seq") % 2


def half(side):
    return slice(side * PAIR, (side + 1) * PAIR)


def pack_body(q_ref, k_ref, v_ref, send_ref):
    side = core_side()
    for own in range(2):

        @pl.when(side == own)
        def _():
            for i, ref in enumerate((q_ref, k_ref, v_ref)):
                send_ref[i] = ref[:, half(1 - own)]


def join_body(q_ref, k_ref, v_ref, got_ref, q_out, kv_out):
    side = core_side()
    for own in range(2):

        @pl.when(side == own)
        def _():
            mine = slice(own * HD, (own + 1) * HD)
            theirs = slice((1 - own) * HD, (2 - own) * HD)
            q_out[mine, :] = q_ref[:, half(own)]
            q_out[theirs, :] = got_ref[0]
            for i, ref in enumerate((k_ref, v_ref)):
                kv_out[i, mine, :] = ref[:, half(own)]
                kv_out[i, theirs, :] = got_ref[i + 1]


def att_dout_body(d0, d1, d2, d3, w_ref, keep_ref, send_ref):
    dout = project((d0, d1, d2, d3), w_ref, shard_owners(), d0.shape[1])
    side = core_side()
    for own in range(2):

        @pl.when(side == own)
        def _():
            keep_ref[...] = dout[:, half(own)]
            send_ref[...] = dout[:, half(1 - own)]


def join_dout_body(q_ref, keep_ref, got_ref, qd_out):
    side = core_side()
    qd_out[0] = q_ref[...]
    for own in range(2):

        @pl.when(side == own)
        def _():
            qd_out[1, own * HD : (own + 1) * HD, :] = keep_ref[...]
            qd_out[1, (1 - own) * HD : (2 - own) * HD, :] = got_ref[...]


def att_rows_body(qd_ref, kv0, kv1, kv2, kv3, kv4, dq_ref, stat_ref):
    chip = (lax.axis_index("seq") // 2) % (lax.axis_size("seq") // 2 // DOCS)
    rows, cols = grid_ids(PAIR, PAIR)
    near = cols <= rows
    scale = 1.0 / math.sqrt(HD)
    blocks = (kv0, kv1, kv2, kv3, kv4)
    lanes = lax.broadcasted_iota(jnp.int32, (PAIR, HD), 1)
    stats = jnp.zeros((PAIR, HD), F32)
    for h in range(2):
        hc = head_cols(h)
        q = qd_ref[0, :, hc]
        dout = qd_ref[1, :, hc]
        raw = [dot(q, kv[0, :, hc], NT) * scale for kv in blocks]
        edge = jnp.where(near, raw[0], jnp.where(chip >= RING, raw[RING], FAR))
        scores = [edge] + [jnp.where(chip >= s, raw[s], FAR) for s in range(1, RING)]
        top = scores[0]
        for part in scores[1:]:
            top = jnp.maximum(top, part)
        top = jnp.max(top, axis=1, keepdims=True)
        expo = [jnp.exp(part - top) for part in scores]
        mass = jnp.sum(expo[0] + expo[1] + expo[2] + expo[3], axis=1, keepdims=True)
        inv = 1.0 / mass
        probs = [e * inv for e in expo]
        dp = [dot(dout, kv[1, :, hc], NT) for kv in blocks]
        dprob = [jnp.where(near, dp[0], dp[RING])] + dp[1:RING]
        spread = probs[0] * dprob[0]
        for s in range(1, RING):
            spread = spread + probs[s] * dprob[s]
        row_dot = jnp.sum(spread, axis=1, keepdims=True)
        dscore = [p * (d - row_dot) for p, d in zip(probs, dprob)]
        grad = dot(jnp.where(near, dscore[0], 0.0).astype(BF16), kv0[0, :, hc], NN)
        grad = grad + dot(jnp.where(near, 0.0, dscore[0]).astype(BF16), kv4[0, :, hc], NN)
        for s in range(1, RING):
            grad = grad + dot(dscore[s].astype(BF16), blocks[s][0, :, hc], NN)
        dq_ref[:, hc] = (grad * scale).astype(BF16)
        for i, col in enumerate((top, inv, row_dot)):
            stats = jnp.where(lanes == 3 * h + i, col, stats)
    stat_ref[...] = stats.T[:8]


def att_cols_body(
    kv_ref, dq_ref, qd0, qd1, qd2, qd3, qd4, st0, st1, st2, st3, st4, keep_ref, send_ref, out_ref
):
    rows, cols = grid_ids(PAIR, PAIR)
    near = rows <= cols
    scale = 1.0 / math.sqrt(HD)
    out_ref[0] = dq_ref[...]
    for h in range(2):
        hc = head_cols(h)
        k = kv_ref[0, :, hc]
        v = kv_ref[1, :, hc]
        dk = jnp.zeros((PAIR, HD), F32)
        dv = jnp.zeros((PAIR, HD), F32)
        for s, (qd, st) in enumerate(zip((qd0, qd1, qd2, qd3, qd4), (st0, st1, st2, st3, st4))):
            q = qd[0, :, hc]
            dout = qd[1, :, hc]
            stats = st[...]
            shifted = dot(k, q, NT) * scale - stats[3 * h : 3 * h + 1]
            if s == 0:
                shifted = jnp.where(near, shifted, FAR)
            if s == RING:
                shifted = jnp.where(near, FAR, shifted)
            probs = jnp.exp(shifted) * stats[3 * h + 1 : 3 * h + 2]
            dscore = probs * (dot(v, dout, NT) - stats[3 * h + 2 : 3 * h + 3])
            dk = dk + dot(dscore.astype(BF16), q, NN)
            dv = dv + dot(probs.astype(BF16), dout, NN)
        out_ref[1, :, hc] = (dk * scale).astype(BF16)
        out_ref[2, :, hc] = dv.astype(BF16)
    side = core_side()
    for own in range(2):

        @pl.when(side == own)
        def _():
            keep_ref[...] = out_ref[:, own * HD : (own + 1) * HD, :]
            send_ref[...] = out_ref[:, (1 - own) * HD : (2 - own) * HD, :]


def finish_body(keep_ref, got_ref, dq_ref, dk_ref, dv_ref):
    side = core_side()
    for own in range(2):

        @pl.when(side == own)
        def _():
            for i, ref in enumerate((dq_ref, dk_ref, dv_ref)):
                ref[:, half(own)] = keep_ref[i]
                ref[:, half(1 - own)] = got_ref[i]


def kernel(body, outs, name, flops=0, scratch=()):
    shapes = [jax.ShapeDtypeStruct(shape, dtype) for shape, dtype in outs]
    nbytes = sum(math.prod(s.shape) * s.dtype.itemsize for s in shapes)
    return pl.pallas_call(
        body,
        out_shape=shapes if len(shapes) > 1 else shapes[0],
        scratch_shapes=list(scratch),
        compiler_params=pltpu.CompilerParams(vmem_limit_bytes=48 * 1024 * 1024),
        cost_estimate=pl.CostEstimate(flops=flops, bytes_accessed=2 * nbytes, transcendentals=0),
        name=name,
    )


def bind(body, **fixed):
    def bound(*refs):
        return body(*refs, **fixed)

    return bound


def shards(
    att_q, att_k, att_v, att_dy, att_out_w,
    gdn_q, gdn_k, gdn_v, gdn_beta, gdn_gate, gdn_state, gdn_dy, gdn_out_w,
):
    toks, width = att_q.shape
    heads = width // HD
    seq_count = lax.axis_size("seq")
    head_count = lax.axis_size("head")
    per_doc = seq_count // DOCS
    swap = [(i, i ^ 1) for i in range(seq_count)]
    forth = [(i, i + 2) for i in range(seq_count - 2) if i // per_doc == (i + 2) // per_doc]
    back = [(j, i) for i, j in forth]

    def gathered(value):
        return [value] + [
            lax.ppermute(value, "head", [(i, (i + s) % head_count) for i in range(head_count)])
            for s in range(1, head_count)
        ]

    gdn_parts = gathered(gdn_dy)
    send = kernel(pack_body, [((3, toks, PAIR), BF16)], "att_pack")(att_q, att_k, att_v)
    got = lax.ppermute(send, "seq", swap)
    att_parts = gathered(att_dy)
    q_pair, kv_pair = kernel(
        join_body, [((PAIR, PAIR), BF16), ((2, PAIR, PAIR), BF16)], "att_join"
    )(att_q, att_k, att_v, got)
    kv = [kv_pair]
    for _ in range(RING):
        kv.append(lax.ppermute(kv[-1], "seq", forth))

    inverse, n_map, delta = kernel(
        bind(gdn_pre_body, heads=heads),
        [((heads, HD, HD), F32), ((heads, HD, HD), F32), ((heads, HD + 16, HD), BF16)],
        "gdn_pre", flops=3 * 10**9,
    )(gdn_q, gdn_k, gdn_beta, gdn_gate)
    gdn_dout, payload = kernel(
        bind(gdn_dout_body, heads=heads),
        [((toks, width), BF16), ((heads, 2 * HD + 16, HD), BF16)],
        "gdn_dout", flops=10**9,
    )(*gdn_parts, gdn_out_w, n_map, delta)

    quads = [[SEG * i + j for j in range(SEG)] for i in range(seq_count // SEG)]
    blocks = lax.all_to_all(payload, "seq", 0, 0, axis_index_groups=quads)
    folded = kernel(chain_fold_body, [((2 * HD + 16, HD), BF16)], "chain_fold")(blocks)
    later = [
        lax.ppermute(
            folded, "seq",
            [(i, i - SEG * s) for i in range(seq_count) if i % per_doc >= SEG * s],
        )
        for s in range(1, SEGS)
    ]
    walked = kernel(chain_walk_body, [((SEG, HD, HD), BF16)], "chain_walk")(*later, blocks)
    adjoint = lax.all_to_all(walked, "seq", 0, 0, axis_index_groups=quads)
    gdn_dq, gdn_dk, gdn_dv, gdn_dbeta, gdn_dgate = kernel(
        bind(gdn_post_body, heads=heads),
        [((toks, width), BF16)] * 3 + [((heads, toks), F32)] * 2,
        "gdn_post", flops=5 * 10**9,
    )(gdn_q, gdn_k, gdn_v, gdn_beta, gdn_gate, gdn_state[0], inverse, gdn_dout, adjoint)

    dout_keep, dout_send = kernel(
        att_dout_body, [((toks, PAIR), BF16)] * 2, "att_dout", flops=10**9
    )(*att_parts, att_out_w)
    dout_got = lax.ppermute(dout_send, "seq", swap)
    qd = [kernel(join_dout_body, [((2, PAIR, PAIR), BF16)], "att_join_dout")(q_pair, dout_keep, dout_got)]
    for _ in range(RING):
        qd.append(lax.ppermute(qd[-1], "seq", back))
    dq_pair, stats = kernel(
        att_rows_body, [((PAIR, PAIR), BF16), ((8, PAIR), F32)], "att_rows", flops=3 * 10**9
    )(qd[0], *kv)
    all_stats = [stats] + [
        lax.ppermute(
            stats, "seq",
            [(i, i - 2 * s) for i in range(seq_count) if i % per_doc >= 2 * s],
        )
        for s in range(1, RING + 1)
    ]
    keep, send = kernel(
        att_cols_body, [((3, toks, PAIR), BF16)] * 2, "att_cols", flops=3 * 10**9,
        scratch=[pltpu.VMEM((3, PAIR, PAIR), BF16)],
    )(kv_pair, dq_pair, *qd, *all_stats)
    got = lax.ppermute(send, "seq", swap)
    att_dq, att_dk, att_dv = kernel(finish_body, [((toks, width), BF16)] * 3, "att_finish")(keep, got)
    return (att_dq, att_dk, att_dv, gdn_dq, gdn_dk, gdn_dv, gdn_dbeta, gdn_dgate)


def solution(mesh):
    tokens = P("seq", "head")
    rates = P("head", "seq")
    weight = P("head", None)
    return jax.shard_map(
        shards,
        mesh=mesh,
        in_specs=(
            tokens, tokens, tokens, tokens, weight,
            tokens, tokens, tokens, rates, rates, P("seq", "head", None, None), tokens, weight,
        ),
        out_specs=(tokens, tokens, tokens, tokens, tokens, tokens, rates, rates),
        check_vma=False,
    )
```

time: 1080 us -> 114 us (0.11); the launches traced: 1060 us -> 113 us
  other arithmetic: 248 us -> 0 us
  waiting for transfers between devices: 246 us -> 8.53 us
  matrix products: 185 us -> 0 us
  starting transfers between devices: 240 us -> 78.4 us
  local copies, waits for them, and re-layouts: 112 us -> 6.85 us
  blocking collectives: 26.8 us -> 0 us
  Pallas kernels: 0 us -> 18.1 us
    ppermute x47 -> x28, waiting for transfers between devices: 246 us -> 8.1 us  [the longest x7 5.72 us: shards(): lax.ppermute(folded, 'seq', [(i, i - SEG * s) for i in range(seq_count) i...]
    another operation x81 -> x0, other arithmetic: 197 us -> none  [the longest x28 129 us: group_step(): lax.linalg.triangular_solve(system, right_side, left_side=True, lower=Tru...]
    ppermute x47 -> x28, starting transfers between devices: 240 us -> 71.6 us  [the longest x4 25.7 us: shards(): qd.append(lax.ppermute(qd[-1], 'seq', back))]
    dot_general x105 -> x0, matrix products: 164 us -> none  [the longest x64 74 us: exact_dot(): return jnp.dot(left, right, precision=lax.Precision.HIGHEST)]
    all_gather x2 -> x0, blocking collectives: 26.8 us -> none  [the longest x1 13.8 us: shards(): lax.all_gather(gdn_dy, 'head', axis=1, tiled=True)]
    slice x20 -> x0, local copies, waits for them, and re-layouts: 23.1 us -> none  [the longest x8 13.4 us: shards(): grad_k[low_row:low_row + tok_rows]]
    reduce_sum x18 -> x0, other arithmetic: 21.5 us -> none  [the longest x4 6.51 us: group_step(): growth[-1] * carried]
    pallas_call x0 -> x12, Pallas kernels: none -> 18.1 us  [the longest x1 4.52 us: shards(): kernel(bind(gdn_post_body, heads=heads), [((toks, width), BF16)] * 3 + [(...]
  transfers between devices with their start and end apart: 47 -> 30, of which waited for: 37 -> 4; matrix products, arithmetic and copies ran while one was open for 48% -> 0% of each run, Pallas kernels for 0% -> 15%
where the time goes in v1:
time: 114 us; the launch traced here: 113 us
  starting transfers between devices  78.4 us (69%)
  Pallas kernels  18.1 us (16%)
  waiting for transfers between devices  8.53 us (7%)
  local copies, waits for them, and re-layouts  6.85 us (6%)
  between operations  1.17 us (1%)
    ppermute x4, starting transfers between devices, shards(): qd.append(lax.ppermute(qd[-1], 'seq', back))  25.7 us
    ppermute x4, starting transfers between devices, shards(): lax.ppermute(stats, 'seq', [(i, i - 2 * s) for i in range(seq_count) if i...  13.4 us
    ppermute x7, starting transfers between devices, shards(): lax.ppermute(folded, 'seq', [(i, i - SEG * s) for i in range(seq_count) i...  11.3 us
    ppermute x6, starting transfers between devices, gathered(): lax.ppermute(value, 'head', [(i, (i + s) % head_count) for i in range(hea...  11.2 us
    ppermute x4, starting transfers between devices, shards(): kv.append(lax.ppermute(kv[-1], 'seq', forth))  9.72 us
    unnamed x34, local copies, waits for them, and re-layouts  6.85 us
    ppermute x7, waiting for transfers between devices, shards(): lax.ppermute(folded, 'seq', [(i, i - SEG * s) for i in range(seq_count) i...  5.72 us
    pallas_call x1, Pallas kernels, shards(): kernel(bind(gdn_post_body, heads=heads), [((toks, width), BF16)] * 3 + [(...  4.52 us
  transfers between devices with their start and end apart: 30, of which 4 were waited for; matrix products, arithmetic and copies ran while one was open for 0% of the time, Pallas kernels for 15%

profile of v1, /device:TPU:6, one launch (start us, length us, event | category | flops | bytes accessed | tf_op | source)
XLA Modules:
  0.0 113.1 jit_solution(9296042515143019761)
XLA Ops:
  5.1 2.9 %collective-permute-start.2 = (bf16[128,512]{1,0:T(8,128)(2,1)}, bf16[128,512]{1,0:T(8,128)(2,1)S(1)}, u32[]{:S(2)}, u32[]{:S(2)}) collective-permute-start(bf16[128,512]{1,0:T(8,128)(2,1)} %d0.1), channel_id=1, source_target_pairs={{0,2},{1,3},{2,0},{3,1},{4,6},{5,7},{6,4},{7,5},{8,10},{9,11},{10,... | collective-permute-start | bytes 393224 | tf_op jit(solution)/shard_map/ppermute | solution.py:434
  9.5 4.0 %collective-permute-start.5 = (bf16[2,256,256]{2,1,0:T(8,128)(2,1)S(1)}, bf16[2,256,256]{2,1,0:T(8,128)(2,1)S(1)}, u32[]{:S(2)}, u32[]{:S(2)}) collective-permute-start(bf16[2,256,256]{2,1,0:T(8,128)(2,1)S(1)} %get-tuple-element.29.kv0.kv_ref), channel_id=1, source_target_pairs={{0,8},{4,12},{8,16},{12,20},{16,24},{20,28},{24,32},{28,36},{32,40... | collective-permute-start | bytes 786440 | tf_op jit(solution)/shard_map/ppermute | solution.py:447
  19.5 2.4 %collective-permute-start.19 = (bf16[128,512]{1,0:T(8,128)(2,1)S(1)}, bf16[128,512]{1,0:T(8,128)(2,1)S(1)}, u32[]{:S(2)}, u32[]{:S(2)}) collective-permute-start(bf16[128,512]{1,0:T(8,128)(2,1)S(1)} %copy-done.7), channel_id=1, source_target_pairs={{0,2},{1,3},{2,0},{3,1},{4,6},{5,7},{6,4},{7,5},{8,10},{9,11},{10,... | collective-permute-start | bytes 393224 | tf_op jit(solution)/shard_map/ppermute | solution.py:434
  23.6 8.2 %collective-permute-start.9 = (bf16[2,256,256]{2,1,0:T(8,128)(2,1)S(1)}, bf16[2,256,256]{2,1,0:T(8,128)(2,1)S(1)}, u32[]{:S(2)}, u32[]{:S(2)}) collective-permute-start(bf16[2,256,256]{2,1,0:T(8,128)(2,1)S(1)} %att_join_dout.1.qd_ref.qd0), channel_id=1, source_target_pairs={{8,0},{12,4},{16,8},{20,12},{24,16},{28,20},{32,24},{36,28},{40,32... | collective-permute-start | bytes 786440 | tf_op jit(solution)/shard_map/ppermute | solution.py:484
  31.8 1.9 %collective-permute-start.6 = (bf16[2,256,256]{2,1,0:T(8,128)(2,1)S(1)}, bf16[2,256,256]{2,1,0:T(8,128)(2,1)S(1)}, u32[]{:S(2)}, u32[]{:S(2)}) collective-permute-start(bf16[2,256,256]{2,1,0:T(8,128)(2,1)S(1)} %collective-permute-done.5.kv1), channel_id=1, source_target_pairs={{0,8},{4,12},{8,16},{12,20},{16,24},{20,28},{24,32},{28,36},{32,40... | collective-permute-start | bytes 786440 | tf_op jit(solution)/shard_map/ppermute | solution.py:447
  33.8 3.4 %gdn_pre.1 = (f32[4,128,128]{2,1,0:T(8,128)S(1)}, f32[4,128,128]{2,1,0:T(8,128)S(1)}, bf16[4,144,128]{2,1,0:T(8,128)(2,1)S(1)}) custom-call(bf16[128,512]{1,0:T(8,128)(2,1)S(1)} %copy-done.8, bf16[128,512]{1,0:T(8,128)(2,1)S(1)} %copy-done.9, f32[4,128]{1,0:T(4,128)S(1)} %copy-done.11, f32[4,128]{1,0:T(4,128)S(1)} %copy-done.12), custom_call_target="tpu_custom_call" | custom-call | flops 3000000000 | bytes 1343488 | tf_op jit(solution)/shard_map/gdn_pre/pallas_call | solution.py:449
  37.9 6.0 %collective-permute-start.10 = (bf16[2,256,256]{2,1,0:T(8,128)(2,1)S(1)}, bf16[2,256,256]{2,1,0:T(8,128)(2,1)S(1)}, u32[]{:S(2)}, u32[]{:S(2)}) collective-permute-start(bf16[2,256,256]{2,1,0:T(8,128)(2,1)S(1)} %collective-permute-done.9.qd1), channel_id=1, source_target_pairs={{8,0},{12,4},{16,8},{20,12},{24,16},{28,20},{32,24},{36,28},{40,32... | collective-permute-start | bytes 786440 | tf_op jit(solution)/shard_map/ppermute | solution.py:484
  43.9 1.9 %collective-permute-start.7 = (bf16[2,256,256]{2,1,0:T(8,128)(2,1)S(1)}, bf16[2,256,256]{2,1,0:T(8,128)(2,1)S(1)}, u32[]{:S(2)}, u32[]{:S(2)}) collective-permute-start(bf16[2,256,256]{2,1,0:T(8,128)(2,1)S(1)} %collective-permute-done.6.kv2), channel_id=1, source_target_pairs={{0,8},{4,12},{8,16},{12,20},{16,24},{20,28},{24,32},{28,36},{32,40... | collective-permute-start | bytes 786440 | tf_op jit(solution)/shard_map/ppermute | solution.py:447
  47.7 3.4 %all-to-all-start = ((bf16[4,272,128]{2,1,0:T(8,128)(2,1)}), bf16[4,272,128]{2,1,0:T(8,128)(2,1)S(1)}, u32[]{:S(2)}, u32[]{:S(2)}) async-start(bf16[4,272,128]{2,1,0:T(8,128)(2,1)} %get-tuple-element.44), calls=%async_computation | async-start | bytes 557056 | tf_op jit(solution)/shard_map/all_to_all | solution.py:461
  51.1 6.0 %collective-permute-start.11 = (bf16[2,256,256]{2,1,0:T(8,128)(2,1)S(1)}, bf16[2,256,256]{2,1,0:T(8,128)(2,1)S(1)}, u32[]{:S(2)}, u32[]{:S(2)}) collective-permute-start(bf16[2,256,256]{2,1,0:T(8,128)(2,1)S(1)} %collective-permute-done.10.qd2), channel_id=1, source_target_pairs={{8,0},{12,4},{16,8},{20,12},{24,16},{28,20},{32,24},{36,28},{40,32... | collective-permute-start | bytes 786440 | tf_op jit(solution)/shard_map/ppermute | solution.py:484
  57.2 1.9 %collective-permute-start.8 = (bf16[2,256,256]{2,1,0:T(8,128)(2,1)S(1)}, bf16[2,256,256]{2,1,0:T(8,128)(2,1)S(1)}, u32[]{:S(2)}, u32[]{:S(2)}) collective-permute-start(bf16[2,256,256]{2,1,0:T(8,128)(2,1)S(1)} %collective-permute-done.7.kv3), channel_id=1, source_target_pairs={{0,8},{4,12},{8,16},{12,20},{16,24},{20,28},{24,32},{28,36},{32,40... | collective-permute-start | bytes 786440 | tf_op jit(solution)/shard_map/ppermute | solution.py:447
  59.6 4.2 %collective-permute-start.21 = (bf16[272,128]{1,0:T(8,128)(2,1)S(1)}, bf16[272,128]{1,0:T(8,128)(2,1)S(1)}, u32[]{:S(2)}, u32[]{:S(2)}) collective-permute-start(bf16[272,128]{1,0:T(8,128)(2,1)S(1)} %chain_fold.1), channel_id=1, source_target_pairs={{16,0},{20,4},{24,8},{28,12},{32,16},{36,20},{40,24},{44,28},{48,3... | collective-permute-start | bytes 208904 | tf_op jit(solution)/shard_map/ppermute | solution.py:464
  63.8 1.9 %collective-permute-start.22 = (bf16[272,128]{1,0:T(8,128)(2,1)S(1)}, bf16[272,128]{1,0:T(8,128)(2,1)S(1)}, u32[]{:S(2)}, u32[]{:S(2)}) collective-permute-start(bf16[272,128]{1,0:T(8,128)(2,1)S(1)} %chain_fold.1), channel_id=1, source_target_pairs={{32,0},{36,4},{40,8},{44,12},{48,16},{52,20},{56,24},{60,28},{64,3... | collective-permute-start | bytes 208904 | tf_op jit(solution)/shard_map/ppermute | solution.py:464
  69.0 5.7 %collective-permute-done.22.refs_1_ = bf16[272,128]{1,0:T(8,128)(2,1)S(1)} collective-permute-done((bf16[272,128]{1,0:T(8,128)(2,1)S(1)}, bf16[272,128]{1,0:T(8,128)(2,1)S(1)}, u32[]{:S(2)}, u32[]{:S(2)}) %collective-permute-start.22) | collective-permute-done | bytes 69664 | tf_op jit(solution)/shard_map/ppermute | solution.py:464
  76.7 5.5 %collective-permute-start.12 = (bf16[2,256,256]{2,1,0:T(8,128)(2,1)S(1)}, bf16[2,256,256]{2,1,0:T(8,128)(2,1)S(1)}, u32[]{:S(2)}, u32[]{:S(2)}) collective-permute-start(bf16[2,256,256]{2,1,0:T(8,128)(2,1)S(1)} %collective-permute-done.11.qd3), channel_id=1, source_target_pairs={{8,0},{12,4},{16,8},{20,12},{24,16},{28,20},{32,24},{36,28},{40,32... | collective-permute-start | bytes 786440 | tf_op jit(solution)/shard_map/ppermute | solution.py:484
  82.2 2.0 %att_rows.1 = (bf16[256,256]{1,0:T(8,128)(2,1)S(1)}, f32[8,256]{1,0:T(8,128)S(1)}) custom-call(bf16[2,256,256]{2,1,0:T(8,128)(2,1)S(1)} %att_join_dout.1.qd_ref.qd0, bf16[2,256,256]{2,1,0:T(8,128)(2,1)S(1)} %get-tuple-element.29.kv0.kv_ref, bf16[2,256,256]{2,1,0:T(8,128)(2,1)S(1)} %collective-permute-done.5.kv1, ...), custom_call_target="tpu_custom_call" | custom-call | flops 3000000000 | bytes 278528 | tf_op jit(solution)/shard_map/att_rows/pallas_call | solution.py:485
  84.3 2.0 %collective-permute-start.13 = (f32[8,256]{1,0:T(8,128)S(1)}, f32[8,256]{1,0:T(8,128)S(1)}, u32[]{:S(2)}, u32[]{:S(2)}) collective-permute-start(f32[8,256]{1,0:T(8,128)S(1)} %get-tuple-element.34.st0), channel_id=1, source_target_pairs={{8,0},{12,4},{16,8},{20,12},{24,16},{28,20},{32,24},{36,28},{40,32... | collective-permute-start | bytes 24584 | tf_op jit(solution)/shard_map/ppermute | solution.py:489
  86.3 2.8 %collective-permute-start.14 = (f32[8,256]{1,0:T(8,128)S(1)}, f32[8,256]{1,0:T(8,128)S(1)}, u32[]{:S(2)}, u32[]{:S(2)}) collective-permute-start(f32[8,256]{1,0:T(8,128)S(1)} %get-tuple-element.34.st0), channel_id=1, source_target_pairs={{16,0},{20,4},{24,8},{28,12},{32,16},{36,20},{40,24},{44,28},{48,3... | collective-permute-start | bytes 24584 | tf_op jit(solution)/shard_map/ppermute | solution.py:489
  89.1 5.5 %collective-permute-start.15 = (f32[8,256]{1,0:T(8,128)S(1)}, f32[8,256]{1,0:T(8,128)S(1)}, u32[]{:S(2)}, u32[]{:S(2)}) collective-permute-start(f32[8,256]{1,0:T(8,128)S(1)} %get-tuple-element.34.st0), channel_id=1, source_target_pairs={{24,0},{28,4},{32,8},{36,12},{40,16},{44,20},{48,24},{52,28},{56,3... | collective-permute-start | bytes 24584 | tf_op jit(solution)/shard_map/ppermute | solution.py:489
  94.7 3.1 %collective-permute-start.16 = (f32[8,256]{1,0:T(8,128)S(1)}, f32[8,256]{1,0:T(8,128)S(1)}, u32[]{:S(2)}, u32[]{:S(2)}) collective-permute-start(f32[8,256]{1,0:T(8,128)S(1)} %get-tuple-element.34.st0), channel_id=1, source_target_pairs={{32,0},{36,4},{40,8},{44,12},{48,16},{52,20},{56,24},{60,28},{64,3... | collective-permute-start | bytes 24584 | tf_op jit(solution)/shard_map/ppermute | solution.py:489
  97.8 2.1 %chain_walk.1 = bf16[4,128,128]{2,1,0:T(8,128)(2,1)} custom-call(bf16[272,128]{1,0:T(8,128)(2,1)S(1)} %collective-permute-done.21.refs_0_, bf16[272,128]{1,0:T(8,128)(2,1)S(1)} %collective-permute-done.22.refs_1_, bf16[272,128]{1,0:T(8,128)(2,1)S(1)} %collective-permute-done.23.refs_2_, bf16[272,128]{1,0:T(8,128)(2,1)S(1)} %collective-permute-done.24.refs_3_, ...), custom_call_target="tpu_custom_call" | custom-call | bytes 262144 | tf_op jit(solution)/shard_map/chain_walk/pallas_call | solution.py:470
  99.8 3.3 %all-to-all-start.1 = ((bf16[4,128,128]{2,1,0:T(8,128)(2,1)}), bf16[4,128,128]{2,1,0:T(8,128)(2,1)S(1)}, u32[]{:S(2)}, u32[]{:S(2)}) async-start(bf16[4,128,128]{2,1,0:T(8,128)(2,1)} %chain_walk.1), calls=%async_computation.1 | async-start | bytes 262144 | tf_op jit(solution)/shard_map/all_to_all | solution.py:471
  105.0 2.2 %att_cols.1 = (bf16[3,128,256]{2,1,0:T(8,128)(2,1)S(1)}, bf16[3,128,256]{2,1,0:T(8,128)(2,1)S(1)}) custom-call(bf16[2,256,256]{2,1,0:T(8,128)(2,1)S(1)} %get-tuple-element.29.kv0.kv_ref, bf16[256,256]{1,0:T(8,128)(2,1)S(1)} %copy-done.16, bf16[2,256,256]{2,1,0:T(8,128)(2,1)S(1)} %att_join_dout.1.qd_ref.qd0, ...), custom_call_target="tpu_custom_call" | custom-call | flops 3000000000 | bytes 786432 | tf_op jit(solution)/shard_map/att_cols/pallas_call | solution.py:495
  107.8 4.5 %gdn_post.1 = (bf16[128,512]{1,0:T(8,128)(2,1)}, bf16[128,512]{1,0:T(8,128)(2,1)}, bf16[128,512]{1,0:T(8,128)(2,1)}, f32[4,128]{1,0:T(4,128)}, f32[4,128]{1,0:T(4,128)}) custom-call(bf16[128,512]{1,0:T(8,128)(2,1)S(1)} %copy-done.8, bf16[128,512]{1,0:T(8,128)(2,1)S(1)} %copy-done.9, bf16[128,512]{1,0:T(8,128)(2,1)S(1)} %copy-done.10, ...), custom_call_target="tpu_custom_call" | custom-call | flops 5000000000 | bytes 794624 | tf_op jit(solution)/shard_map/gdn_post/pallas_call | solution.py:472
  (82 shorter events, 25.0 us)
Async XLA Ops:
  3.5 10.0 %collective-permute-start.1 = (bf16[128,512]{1,0:T(8,128)(2,1)}, bf16[128,512]{1,0:T(8,128)(2,1)S(1)}, u32[]{:S(2)}, u32[]{:S(2)}) collective-permute-start(bf16[128,512]{1,0:T(8,128)(2,1)} %d0.1), channel_id=1, source_target_pairs={{0,1},{1,2},{2,3},{3,0},{4,5},{5,6},{6,7},{7,4},{8,9},{9,10},{10,1... | collective-permute-start | bytes 393224 | tf_op jit(solution)/shard_map/ppermute | solution.py:434
  5.1 9.7 %collective-permute-start.2 = (bf16[128,512]{1,0:T(8,128)(2,1)}, bf16[128,512]{1,0:T(8,128)(2,1)S(1)}, u32[]{:S(2)}, u32[]{:S(2)}) collective-permute-start(bf16[128,512]{1,0:T(8,128)(2,1)} %d0.1), channel_id=1, source_target_pairs={{0,2},{1,3},{2,0},{3,1},{4,6},{5,7},{6,4},{7,5},{8,10},{9,11},{10,... | collective-permute-start | bytes 393224 | tf_op jit(solution)/shard_map/ppermute | solution.py:434
  9.5 22.3 %collective-permute-start.5 = (bf16[2,256,256]{2,1,0:T(8,128)(2,1)S(1)}, bf16[2,256,256]{2,1,0:T(8,128)(2,1)S(1)}, u32[]{:S(2)}, u32[]{:S(2)}) collective-permute-start(bf16[2,256,256]{2,1,0:T(8,128)(2,1)S(1)} %get-tuple-element.29.kv0.kv_ref), channel_id=1, source_target_pairs={{0,8},{4,12},{8,16},{12,20},{16,24},{20,28},{24,32},{28,36},{32,40... | collective-permute-start | bytes 786440 | tf_op jit(solution)/shard_map/ppermute | solution.py:447
  18.3 27.5 %collective-permute-start.18 = (bf16[128,512]{1,0:T(8,128)(2,1)S(1)}, bf16[128,512]{1,0:T(8,128)(2,1)S(1)}, u32[]{:S(2)}, u32[]{:S(2)}) collective-permute-start(bf16[128,512]{1,0:T(8,128)(2,1)S(1)} %copy-done.7), channel_id=1, source_target_pairs={{0,1},{1,2},{2,3},{3,0},{4,5},{5,6},{6,7},{7,4},{8,9},{9,10},{10,1... | collective-permute-start | bytes 393224 | tf_op jit(solution)/shard_map/ppermute | solution.py:434
  19.5 26.4 %collective-permute-start.19 = (bf16[128,512]{1,0:T(8,128)(2,1)S(1)}, bf16[128,512]{1,0:T(8,128)(2,1)S(1)}, u32[]{:S(2)}, u32[]{:S(2)}) collective-permute-start(bf16[128,512]{1,0:T(8,128)(2,1)S(1)} %copy-done.7), channel_id=1, source_target_pairs={{0,2},{1,3},{2,0},{3,1},{4,6},{5,7},{6,4},{7,5},{8,10},{9,11},{10,... | collective-permute-start | bytes 393224 | tf_op jit(solution)/shard_map/ppermute | solution.py:434
  21.9 24.0 %collective-permute-start.20 = (bf16[128,512]{1,0:T(8,128)(2,1)S(1)}, bf16[128,512]{1,0:T(8,128)(2,1)S(1)}, u32[]{:S(2)}, u32[]{:S(2)}) collective-permute-start(bf16[128,512]{1,0:T(8,128)(2,1)S(1)} %copy-done.7), channel_id=1, source_target_pairs={{0,3},{1,0},{2,1},{3,2},{4,7},{5,4},{6,5},{7,6},{8,11},{9,8},{10,9... | collective-permute-start | bytes 393224 | tf_op jit(solution)/shard_map/ppermute | solution.py:434
  23.6 14.2 %collective-permute-start.9 = (bf16[2,256,256]{2,1,0:T(8,128)(2,1)S(1)}, bf16[2,256,256]{2,1,0:T(8,128)(2,1)S(1)}, u32[]{:S(2)}, u32[]{:S(2)}) collective-permute-start(bf16[2,256,256]{2,1,0:T(8,128)(2,1)S(1)} %att_join_dout.1.qd_ref.qd0), channel_id=1, source_target_pairs={{8,0},{12,4},{16,8},{20,12},{24,16},{28,20},{32,24},{36,28},{40,32... | collective-permute-start | bytes 786440 | tf_op jit(solution)/shard_map/ppermute | solution.py:484
  31.8 12.1 %collective-permute-start.6 = (bf16[2,256,256]{2,1,0:T(8,128)(2,1)S(1)}, bf16[2,256,256]{2,1,0:T(8,128)(2,1)S(1)}, u32[]{:S(2)}, u32[]{:S(2)}) collective-permute-start(bf16[2,256,256]{2,1,0:T(8,128)(2,1)S(1)} %collective-permute-done.5.kv1), channel_id=1, source_target_pairs={{0,8},{4,12},{8,16},{12,20},{16,24},{20,28},{24,32},{28,36},{32,40... | collective-permute-start | bytes 786440 | tf_op jit(solution)/shard_map/ppermute | solution.py:447
  37.9 13.2 %collective-permute-start.10 = (bf16[2,256,256]{2,1,0:T(8,128)(2,1)S(1)}, bf16[2,256,256]{2,1,0:T(8,128)(2,1)S(1)}, u32[]{:S(2)}, u32[]{:S(2)}) collective-permute-start(bf16[2,256,256]{2,1,0:T(8,128)(2,1)S(1)} %collective-permute-done.9.qd1), channel_id=1, source_target_pairs={{8,0},{12,4},{16,8},{20,12},{24,16},{28,20},{32,24},{36,28},{40,32... | collective-permute-start | bytes 786440 | tf_op jit(solution)/shard_map/ppermute | solution.py:484
  43.9 13.2 %collective-permute-start.7 = (bf16[2,256,256]{2,1,0:T(8,128)(2,1)S(1)}, bf16[2,256,256]{2,1,0:T(8,128)(2,1)S(1)}, u32[]{:S(2)}, u32[]{:S(2)}) collective-permute-start(bf16[2,256,256]{2,1,0:T(8,128)(2,1)S(1)} %collective-permute-done.6.kv2), channel_id=1, source_target_pairs={{0,8},{4,12},{8,16},{12,20},{16,24},{20,28},{24,32},{28,36},{32,40... | collective-permute-start | bytes 786440 | tf_op jit(solution)/shard_map/ppermute | solution.py:447
  47.7 11.4 %all-to-all-start = ((bf16[4,272,128]{2,1,0:T(8,128)(2,1)}), bf16[4,272,128]{2,1,0:T(8,128)(2,1)S(1)}, u32[]{:S(2)}, u32[]{:S(2)}) async-start(bf16[4,272,128]{2,1,0:T(8,128)(2,1)} %get-tuple-element.44), calls=%async_computation | async-start | bytes 557056 | tf_op jit(solution)/shard_map/all_to_all | solution.py:461
  51.1 24.9 %collective-permute-start.11 = (bf16[2,256,256]{2,1,0:T(8,128)(2,1)S(1)}, bf16[2,256,256]{2,1,0:T(8,128)(2,1)S(1)}, u32[]{:S(2)}, u32[]{:S(2)}) collective-permute-start(bf16[2,256,256]{2,1,0:T(8,128)(2,1)S(1)} %collective-permute-done.10.qd2), channel_id=1, source_target_pairs={{8,0},{12,4},{16,8},{20,12},{24,16},{28,20},{32,24},{36,28},{40,32... | collective-permute-start | bytes 786440 | tf_op jit(solution)/shard_map/ppermute | solution.py:484
  57.2 19.5 %collective-permute-start.8 = (bf16[2,256,256]{2,1,0:T(8,128)(2,1)S(1)}, bf16[2,256,256]{2,1,0:T(8,128)(2,1)S(1)}, u32[]{:S(2)}, u32[]{:S(2)}) collective-permute-start(bf16[2,256,256]{2,1,0:T(8,128)(2,1)S(1)} %collective-permute-done.7.kv3), channel_id=1, source_target_pairs={{0,8},{4,12},{8,16},{12,20},{16,24},{20,28},{24,32},{28,36},{32,40... | collective-permute-start | bytes 786440 | tf_op jit(solution)/shard_map/ppermute | solution.py:447
  63.8 10.9 %collective-permute-start.22 = (bf16[272,128]{1,0:T(8,128)(2,1)S(1)}, bf16[272,128]{1,0:T(8,128)(2,1)S(1)}, u32[]{:S(2)}, u32[]{:S(2)}) collective-permute-start(bf16[272,128]{1,0:T(8,128)(2,1)S(1)} %chain_fold.1), channel_id=1, source_target_pairs={{32,0},{36,4},{40,8},{44,12},{48,16},{52,20},{56,24},{60,28},{64,3... | collective-permute-start | bytes 208904 | tf_op jit(solution)/shard_map/ppermute | solution.py:464
  65.7 9.6 %collective-permute-start.23 = (bf16[272,128]{1,0:T(8,128)(2,1)S(1)}, bf16[272,128]{1,0:T(8,128)(2,1)S(1)}, u32[]{:S(2)}, u32[]{:S(2)}) collective-permute-start(bf16[272,128]{1,0:T(8,128)(2,1)S(1)} %chain_fold.1), channel_id=1, source_target_pairs={{48,0},{52,4},{56,8},{60,12},{64,16},{68,20},{72,24},{76,28},{80,3... | collective-permute-start | bytes 208904 | tf_op jit(solution)/shard_map/ppermute | solution.py:464
  67.7 16.6 %collective-permute-start.24 = (bf16[272,128]{1,0:T(8,128)(2,1)S(1)}, bf16[272,128]{1,0:T(8,128)(2,1)S(1)}, u32[]{:S(2)}, u32[]{:S(2)}) collective-permute-start(bf16[272,128]{1,0:T(8,128)(2,1)S(1)} %chain_fold.1), channel_id=1, source_target_pairs={{64,0},{68,4},{72,8},{76,12},{80,16},{84,20},{88,24},{92,28},{96,3... | collective-permute-start | bytes 208904 | tf_op jit(solution)/shard_map/ppermute | solution.py:464
  74.7 11.7 %collective-permute-start.25 = (bf16[272,128]{1,0:T(8,128)(2,1)S(1)}, bf16[272,128]{1,0:T(8,128)(2,1)S(1)}, u32[]{:S(2)}, u32[]{:S(2)}) collective-permute-start(bf16[272,128]{1,0:T(8,128)(2,1)S(1)} %chain_fold.1), channel_id=1, source_target_pairs={{80,0},{84,4},{88,8},{92,12},{96,16},{100,20},{104,24},{108,28},{1... | collective-permute-start | bytes 208904 | tf_op jit(solution)/shard_map/ppermute | solution.py:464
  75.3 13.8 %collective-permute-start.26 = (bf16[272,128]{1,0:T(8,128)(2,1)S(1)}, bf16[272,128]{1,0:T(8,128)(2,1)S(1)}, u32[]{:S(2)}, u32[]{:S(2)}) collective-permute-start(bf16[272,128]{1,0:T(8,128)(2,1)S(1)} %chain_fold.1), channel_id=1, source_target_pairs={{96,0},{100,4},{104,8},{108,12},{112,16},{116,20},{120,24},{124,28... | collective-permute-start | bytes 208904 | tf_op jit(solution)/shard_map/ppermute | solution.py:464
  76.0 18.6 %collective-permute-start.27 = (bf16[272,128]{1,0:T(8,128)(2,1)S(1)}, bf16[272,128]{1,0:T(8,128)(2,1)S(1)}, u32[]{:S(2)}, u32[]{:S(2)}) collective-permute-start(bf16[272,128]{1,0:T(8,128)(2,1)S(1)} %chain_fold.1), channel_id=1, source_target_pairs={{112,0},{116,4},{120,8},{124,12},{240,128},{244,132},{248,136},{25... | collective-permute-start | bytes 208904 | tf_op jit(solution)/shard_map/ppermute | solution.py:464
  76.7 26.5 %collective-permute-start.12 = (bf16[2,256,256]{2,1,0:T(8,128)(2,1)S(1)}, bf16[2,256,256]{2,1,0:T(8,128)(2,1)S(1)}, u32[]{:S(2)}, u32[]{:S(2)}) collective-permute-start(bf16[2,256,256]{2,1,0:T(8,128)(2,1)S(1)} %collective-permute-done.11.qd3), channel_id=1, source_target_pairs={{8,0},{12,4},{16,8},{20,12},{24,16},{28,20},{32,24},{36,28},{40,32... | collective-permute-start | bytes 786440 | tf_op jit(solution)/shard_map/ppermute | solution.py:484
  84.3 18.9 %collective-permute-start.13 = (f32[8,256]{1,0:T(8,128)S(1)}, f32[8,256]{1,0:T(8,128)S(1)}, u32[]{:S(2)}, u32[]{:S(2)}) collective-permute-start(f32[8,256]{1,0:T(8,128)S(1)} %get-tuple-element.34.st0), channel_id=1, source_target_pairs={{8,0},{12,4},{16,8},{20,12},{24,16},{28,20},{32,24},{36,28},{40,32... | collective-permute-start | bytes 24584 | tf_op jit(solution)/shard_map/ppermute | solution.py:489
  86.3 16.9 %collective-permute-start.14 = (f32[8,256]{1,0:T(8,128)S(1)}, f32[8,256]{1,0:T(8,128)S(1)}, u32[]{:S(2)}, u32[]{:S(2)}) collective-permute-start(f32[8,256]{1,0:T(8,128)S(1)} %get-tuple-element.34.st0), channel_id=1, source_target_pairs={{16,0},{20,4},{24,8},{28,12},{32,16},{36,20},{40,24},{44,28},{48,3... | collective-permute-start | bytes 24584 | tf_op jit(solution)/shard_map/ppermute | solution.py:489
  89.1 14.1 %collective-permute-start.15 = (f32[8,256]{1,0:T(8,128)S(1)}, f32[8,256]{1,0:T(8,128)S(1)}, u32[]{:S(2)}, u32[]{:S(2)}) collective-permute-start(f32[8,256]{1,0:T(8,128)S(1)} %get-tuple-element.34.st0), channel_id=1, source_target_pairs={{24,0},{28,4},{32,8},{36,12},{40,16},{44,20},{48,24},{52,28},{56,3... | collective-permute-start | bytes 24584 | tf_op jit(solution)/shard_map/ppermute | solution.py:489
  94.7 9.5 %collective-permute-start.16 = (f32[8,256]{1,0:T(8,128)S(1)}, f32[8,256]{1,0:T(8,128)S(1)}, u32[]{:S(2)}, u32[]{:S(2)}) collective-permute-start(f32[8,256]{1,0:T(8,128)S(1)} %get-tuple-element.34.st0), channel_id=1, source_target_pairs={{32,0},{36,4},{40,8},{44,12},{48,16},{52,20},{56,24},{60,28},{64,3... | collective-permute-start | bytes 24584 | tf_op jit(solution)/shard_map/ppermute | solution.py:489
  (23 other events, 208.9 us)

commit v2 on v1

--- a/solution.py
+++ b/solution.py
@@ -10,8 +10,8 @@
 HD = 128
 PAIR = 256
 RING = 4
-SEG = 4
-SEGS = 8
+SEG = 8
+SEGS = 4
 DOCS = 2
 F32 = jnp.float32
 BF16 = jnp.bfloat16
@@ -135,9 +135,13 @@
 def gdn_dout_body(d0, d1, d2, d3, w_ref, n_ref, delta_ref, dout_ref, send_ref, *, heads):
     dout = project((d0, d1, d2, d3), w_ref, shard_owners(), d0.shape[1])
     dout_ref[...] = dout
+    part = HD * heads // SEG
     for h in range(heads):
-        send_ref[h, : HD + 16, :] = delta_ref[h]
-        send_ref[h, HD + 16 :, :] = dot_r(dout[:, head_cols(h)], n_ref[h], TN).astype(BF16)
+        local = dot_r(dout[:, head_cols(h)], n_ref[h], TN).astype(BF16)
+        for i in range(HD // part):
+            slot = h * (HD // part) + i
+            send_ref[slot, : HD + 16, :] = delta_ref[h]
+            send_ref[slot, HD + 16 :, :] = local[i * part : (i + 1) * part]
 
 
 def unpack_map(payload):
@@ -170,13 +174,14 @@
 
 def chain_walk_body(*refs):
     later, blocks_ref, out_ref = refs[: SEGS - 1], refs[SEGS - 1], refs[SEGS]
-    adjoint = jnp.zeros((HD, HD), F32)
+    part = out_ref.shape[1]
+    adjoint = jnp.zeros((part, HD), F32)
 
     def step(adjoint, payload):
         gain, delta, local = unpack_map(payload)
         high, low = split(adjoint)
         both = dot(jnp.concatenate([high, low]), delta, NN)
-        return gain * adjoint - (both[:HD] + both[HD:]) + local
+        return gain * adjoint - (both[:part] + both[part:]) + local
 
     for seg in range(SEGS - 2, -1, -1):
         adjoint = step(adjoint, later[seg][...])
@@ -453,13 +458,13 @@
     )(gdn_q, gdn_k, gdn_beta, gdn_gate)
     gdn_dout, payload = kernel(
         bind(gdn_dout_body, heads=heads),
-        [((toks, width), BF16), ((heads, 2 * HD + 16, HD), BF16)],
+        [((toks, width), BF16), ((SEG, HD + 16 + HD * heads // SEG, HD), BF16)],
         "gdn_dout", flops=10**9,
     )(*gdn_parts, gdn_out_w, n_map, delta)
 
     quads = [[SEG * i + j for j in range(SEG)] for i in range(seq_count // SEG)]
     blocks = lax.all_to_all(payload, "seq", 0, 0, axis_index_groups=quads)
-    folded = kernel(chain_fold_body, [((2 * HD + 16, HD), BF16)], "chain_fold")(blocks)
+    folded = kernel(chain_fold_body, [(blocks.shape[1:], BF16)], "chain_fold")(blocks)
     later = [
         lax.ppermute(
             folded, "seq",
@@ -467,8 +472,8 @@
         )
         for s in range(1, SEGS)
     ]
-    walked = kernel(chain_walk_body, [((SEG, HD, HD), BF16)], "chain_walk")(*later, blocks)
-    adjoint = lax.all_to_all(walked, "seq", 0, 0, axis_index_groups=quads)
+    walked = kernel(chain_walk_body, [((SEG, HD * heads // SEG, HD), BF16)], "chain_walk")(*later, blocks)
+    adjoint = lax.all_to_all(walked, "seq", 0, 0, axis_index_groups=quads).reshape(heads, HD, HD)
     gdn_dq, gdn_dk, gdn_dv, gdn_dbeta, gdn_dgate = kernel(
         bind(gdn_post_body, heads=heads),
         [((toks, width), BF16)] * 3 + [((heads, toks), F32)] * 2,

time: 114 us -> 109 us (0.956)
  starting transfers between devices: 78.4 us -> 68.4 us
  waiting for transfers between devices: 8.53 us -> 12.8 us
    ppermute x4, waiting for transfers between devices: 0.01 us -> 8.47 us  [shards(): qd.append(lax.ppermute(qd[-1], 'seq', back))]
    ppermute x4, starting transfers between devices: 25.7 us -> 17.4 us  [shards(): qd.append(lax.ppermute(qd[-1], 'seq', back))]
    ppermute x7 -> x3, waiting for transfers between devices: 5.72 us -> 0.01 us  [shards(): lax.ppermute(folded, 'seq', [(i, i - SEG * s) for i in range(seq_count) i...]
    ppermute x7 -> x3, starting transfers between devices: 11.3 us -> 6.68 us  [shards(): lax.ppermute(folded, 'seq', [(i, i - SEG * s) for i in range(seq_count) i...]
    ppermute x4, starting transfers between devices: 9.72 us -> 12.5 us  [shards(): kv.append(lax.ppermute(kv[-1], 'seq', forth))]
    all_to_all x1, starting transfers between devices: 3.45 us -> 5.84 us  [shards(): blocks = lax.all_to_all(payload, 'seq', 0, 0, axis_index_groups=quads)]
    all_to_all x1, waiting for transfers between devices: 0.43 us -> 2.52 us  [shards(): lax.all_to_all(walked, 'seq', 0, 0, axis_index_groups=quads)]
    ppermute x6, starting transfers between devices: 11.2 us -> 9.44 us  [gathered(): lax.ppermute(value, 'head', [(i, (i + s) % head_count) for i in range(hea...]
  transfers between devices with their start and end apart: 30 -> 26, of which waited for: 4 -> 4; matrix products, arithmetic and copies ran while one was open for 0% -> 0% of each run, Pallas kernels for 15% -> 17%
where the time goes in v2:
time: 109 us; the launch traced here: 108 us
  starting transfers between devices  68.4 us (63%)
  Pallas kernels  18.7 us (17%)
  waiting for transfers between devices  12.8 us (12%)
  local copies, waits for them, and re-layouts  6.89 us (6%)
  between operations  1.13 us (1%)
    ppermute x4, starting transfers between devices, shards(): qd.append(lax.ppermute(qd[-1], 'seq', back))  17.4 us
    ppermute x4, starting transfers between devices, shards(): kv.append(lax.ppermute(kv[-1], 'seq', forth))  12.5 us
    ppermute x4, starting transfers between devices, shards(): lax.ppermute(stats, 'seq', [(i, i - 2 * s) for i in range(seq_count) if i...  11.7 us
    ppermute x6, starting transfers between devices, gathered(): lax.ppermute(value, 'head', [(i, (i + s) % head_count) for i in range(hea...  9.44 us
    ppermute x4, waiting for transfers between devices, shards(): qd.append(lax.ppermute(qd[-1], 'seq', back))  8.47 us
    unnamed x44, local copies, waits for them, and re-layouts  6.89 us
    ppermute x3, starting transfers between devices, shards(): lax.ppermute(folded, 'seq', [(i, i - SEG * s) for i in range(seq_count) i...  6.68 us
    all_to_all x1, starting transfers between devices, shards(): blocks = lax.all_to_all(payload, 'seq', 0, 0, axis_index_groups=quads)  5.84 us
  transfers between devices with their start and end apart: 26, of which 4 were waited for; matrix products, arithmetic and copies ran while one was open for 0% of the time, Pallas kernels for 17%

profile of v2, /device:TPU:6, one launch (start us, length us, event | category | flops | bytes accessed | tf_op | source)
XLA Modules:
  0.0 108.0 jit_solution(8830648670146808819)
XLA Ops:
  2.3 2.9 %collective-permute-start.2 = (bf16[128,512]{1,0:T(8,128)(2,1)}, bf16[128,512]{1,0:T(8,128)(2,1)S(1)}, u32[]{:S(2)}, u32[]{:S(2)}) collective-permute-start(bf16[128,512]{1,0:T(8,128)(2,1)} %d0.1), channel_id=1, source_target_pairs={{0,2},{1,3},{2,0},{3,1},{4,6},{5,7},{6,4},{7,5},{8,10},{9,11},{10,... | collective-permute-start | bytes 393224 | tf_op jit(solution)/shard_map/ppermute | solution.py:439
  10.2 2.0 %collective-permute-start.19 = (bf16[128,512]{1,0:T(8,128)(2,1)}, bf16[128,512]{1,0:T(8,128)(2,1)S(1)}, u32[]{:S(2)}, u32[]{:S(2)}) collective-permute-start(bf16[128,512]{1,0:T(8,128)(2,1)} %refs_0_.4), channel_id=1, source_target_pairs={{0,2},{1,3},{2,0},{3,1},{4,6},{5,7},{6,4},{7,5},{8,10},{9,11},{10,... | collective-permute-start | bytes 393224 | tf_op jit(solution)/shard_map/ppermute | solution.py:439
  16.5 4.0 %collective-permute-start.5 = (bf16[2,256,256]{2,1,0:T(8,128)(2,1)S(1)}, bf16[2,256,256]{2,1,0:T(8,128)(2,1)S(1)}, u32[]{:S(2)}, u32[]{:S(2)}) collective-permute-start(bf16[2,256,256]{2,1,0:T(8,128)(2,1)S(1)} %get-tuple-element.29.kv0.kv_ref), channel_id=1, source_target_pairs={{0,8},{4,12},{8,16},{12,20},{16,24},{20,28},{24,32},{28,36},{32,40... | collective-permute-start | bytes 786440 | tf_op jit(solution)/shard_map/ppermute | solution.py:452
  20.5 3.4 %gdn_pre.1 = (f32[4,128,128]{2,1,0:T(8,128)S(1)}, f32[4,128,128]{2,1,0:T(8,128)S(1)}, bf16[4,144,128]{2,1,0:T(8,128)(2,1)S(1)}) custom-call(bf16[128,512]{1,0:T(8,128)(2,1)S(1)} %copy-done.11, bf16[128,512]{1,0:T(8,128)(2,1)S(1)} %copy-done.12, f32[4,128]{1,0:T(4,128)S(1)} %copy-done.14, f32[4,128]{1,0:T(4,128)S(1)} %copy-done.15), custom_call_target="tpu_custom_call" | custom-call | flops 3000000000 | bytes 1343488 | tf_op jit(solution)/shard_map/gdn_pre/pallas_call | solution.py:454
  24.7 6.1 %collective-permute-start.9 = (bf16[2,256,256]{2,1,0:T(8,128)(2,1)S(1)}, bf16[2,256,256]{2,1,0:T(8,128)(2,1)S(1)}, u32[]{:S(2)}, u32[]{:S(2)}) collective-permute-start(bf16[2,256,256]{2,1,0:T(8,128)(2,1)S(1)} %att_join_dout.1.qd_ref.qd0), channel_id=1, source_target_pairs={{8,0},{12,4},{16,8},{20,12},{24,16},{28,20},{32,24},{36,28},{40,32... | collective-permute-start | bytes 786440 | tf_op jit(solution)/shard_map/ppermute | solution.py:489
  31.6 1.9 %collective-permute-start.6 = (bf16[2,256,256]{2,1,0:T(8,128)(2,1)S(1)}, bf16[2,256,256]{2,1,0:T(8,128)(2,1)S(1)}, u32[]{:S(2)}, u32[]{:S(2)}) collective-permute-start(bf16[2,256,256]{2,1,0:T(8,128)(2,1)S(1)} %collective-permute-done.5.kv1), channel_id=1, source_target_pairs={{0,8},{4,12},{8,16},{12,20},{16,24},{20,28},{24,32},{28,36},{32,40... | collective-permute-start | bytes 786440 | tf_op jit(solution)/shard_map/ppermute | solution.py:452
  35.4 5.8 %all-to-all-start = ((bf16[8,208,128]{2,1,0:T(8,128)(2,1)}), bf16[8,208,128]{2,1,0:T(8,128)(2,1)S(1)}, u32[]{:S(2)}, u32[]{:S(2)}) async-start(bf16[8,208,128]{2,1,0:T(8,128)(2,1)} %get-tuple-element.44), calls=%async_computation | async-start | bytes 851968 | tf_op jit(solution)/shard_map/all_to_all | solution.py:466
  41.3 5.3 %collective-permute-start.10 = (bf16[2,256,256]{2,1,0:T(8,128)(2,1)S(1)}, bf16[2,256,256]{2,1,0:T(8,128)(2,1)S(1)}, u32[]{:S(2)}, u32[]{:S(2)}) collective-permute-start(bf16[2,256,256]{2,1,0:T(8,128)(2,1)S(1)} %collective-permute-done.9.qd1), channel_id=1, source_target_pairs={{8,0},{12,4},{16,8},{20,12},{24,16},{28,20},{32,24},{36,28},{40,32... | collective-permute-start | bytes 786440 | tf_op jit(solution)/shard_map/ppermute | solution.py:489
  46.6 1.9 %collective-permute-start.7 = (bf16[2,256,256]{2,1,0:T(8,128)(2,1)S(1)}, bf16[2,256,256]{2,1,0:T(8,128)(2,1)S(1)}, u32[]{:S(2)}, u32[]{:S(2)}) collective-permute-start(bf16[2,256,256]{2,1,0:T(8,128)(2,1)S(1)} %collective-permute-done.6.kv2), channel_id=1, source_target_pairs={{0,8},{4,12},{8,16},{12,20},{16,24},{20,28},{24,32},{28,36},{32,40... | collective-permute-start | bytes 786440 | tf_op jit(solution)/shard_map/ppermute | solution.py:452
  48.5 8.5 %collective-permute-done.10.qd2 = bf16[2,256,256]{2,1,0:T(8,128)(2,1)S(1)} collective-permute-done((bf16[2,256,256]{2,1,0:T(8,128)(2,1)S(1)}, bf16[2,256,256]{2,1,0:T(8,128)(2,1)S(1)}, u32[]{:S(2)}, u32[]{:S(2)}) %collective-permute-start.10) | collective-permute-done | bytes 262176 | tf_op jit(solution)/shard_map/ppermute | solution.py:489
  57.0 2.9 %collective-permute-start.11 = (bf16[2,256,256]{2,1,0:T(8,128)(2,1)S(1)}, bf16[2,256,256]{2,1,0:T(8,128)(2,1)S(1)}, u32[]{:S(2)}, u32[]{:S(2)}) collective-permute-start(bf16[2,256,256]{2,1,0:T(8,128)(2,1)S(1)} %collective-permute-done.10.qd2), channel_id=1, source_target_pairs={{8,0},{12,4},{16,8},{20,12},{24,16},{28,20},{32,24},{36,28},{40,32... | collective-permute-start | bytes 786440 | tf_op jit(solution)/shard_map/ppermute | solution.py:489
  59.9 4.7 %collective-permute-start.8 = (bf16[2,256,256]{2,1,0:T(8,128)(2,1)S(1)}, bf16[2,256,256]{2,1,0:T(8,128)(2,1)S(1)}, u32[]{:S(2)}, u32[]{:S(2)}) collective-permute-start(bf16[2,256,256]{2,1,0:T(8,128)(2,1)S(1)} %collective-permute-done.7.kv3), channel_id=1, source_target_pairs={{0,8},{4,12},{8,16},{12,20},{16,24},{20,28},{24,32},{28,36},{32,40... | collective-permute-start | bytes 786440 | tf_op jit(solution)/shard_map/ppermute | solution.py:452
  65.7 4.7 %collective-permute-start.21 = (bf16[208,128]{1,0:T(8,128)(2,1)S(1)}, bf16[208,128]{1,0:T(8,128)(2,1)S(1)}, u32[]{:S(2)}, u32[]{:S(2)}) collective-permute-start(bf16[208,128]{1,0:T(8,128)(2,1)S(1)} %chain_fold.1), channel_id=1, source_target_pairs={{32,0},{36,4},{40,8},{44,12},{48,16},{52,20},{56,24},{60,28},{64,3... | collective-permute-start | bytes 159752 | tf_op jit(solution)/shard_map/ppermute | solution.py:469
  72.4 3.1 %collective-permute-start.12 = (bf16[2,256,256]{2,1,0:T(8,128)(2,1)S(1)}, bf16[2,256,256]{2,1,0:T(8,128)(2,1)S(1)}, u32[]{:S(2)}, u32[]{:S(2)}) collective-permute-start(bf16[2,256,256]{2,1,0:T(8,128)(2,1)S(1)} %collective-permute-done.11.qd3), channel_id=1, source_target_pairs={{8,0},{12,4},{16,8},{20,12},{24,16},{28,20},{32,24},{36,28},{40,32... | collective-permute-start | bytes 786440 | tf_op jit(solution)/shard_map/ppermute | solution.py:489
  75.5 2.0 %att_rows.1 = (bf16[256,256]{1,0:T(8,128)(2,1)S(1)}, f32[8,256]{1,0:T(8,128)S(1)}) custom-call(bf16[2,256,256]{2,1,0:T(8,128)(2,1)S(1)} %att_join_dout.1.qd_ref.qd0, bf16[2,256,256]{2,1,0:T(8,128)(2,1)S(1)} %get-tuple-element.29.kv0.kv_ref, bf16[2,256,256]{2,1,0:T(8,128)(2,1)S(1)} %collective-permute-done.5.kv1, ...), custom_call_target="tpu_custom_call" | custom-call | flops 3000000000 | bytes 278528 | tf_op jit(solution)/shard_map/att_rows/pallas_call | solution.py:490
  77.6 3.9 %collective-permute-start.13 = (f32[8,256]{1,0:T(8,128)S(1)}, f32[8,256]{1,0:T(8,128)S(1)}, u32[]{:S(2)}, u32[]{:S(2)}) collective-permute-start(f32[8,256]{1,0:T(8,128)S(1)} %get-tuple-element.34.st0), channel_id=1, source_target_pairs={{8,0},{12,4},{16,8},{20,12},{24,16},{28,20},{32,24},{36,28},{40,32... | collective-permute-start | bytes 24584 | tf_op jit(solution)/shard_map/ppermute | solution.py:494
  81.5 3.4 %collective-permute-start.14 = (f32[8,256]{1,0:T(8,128)S(1)}, f32[8,256]{1,0:T(8,128)S(1)}, u32[]{:S(2)}, u32[]{:S(2)}) collective-permute-start(f32[8,256]{1,0:T(8,128)S(1)} %get-tuple-element.34.st0), channel_id=1, source_target_pairs={{16,0},{20,4},{24,8},{28,12},{32,16},{36,20},{40,24},{44,28},{48,3... | collective-permute-start | bytes 24584 | tf_op jit(solution)/shard_map/ppermute | solution.py:494
  84.9 2.5 %collective-permute-start.15 = (f32[8,256]{1,0:T(8,128)S(1)}, f32[8,256]{1,0:T(8,128)S(1)}, u32[]{:S(2)}, u32[]{:S(2)}) collective-permute-start(f32[8,256]{1,0:T(8,128)S(1)} %get-tuple-element.34.st0), channel_id=1, source_target_pairs={{24,0},{28,4},{32,8},{36,12},{40,16},{44,20},{48,24},{52,28},{56,3... | collective-permute-start | bytes 24584 | tf_op jit(solution)/shard_map/ppermute | solution.py:494
  87.4 1.9 %collective-permute-start.16 = (f32[8,256]{1,0:T(8,128)S(1)}, f32[8,256]{1,0:T(8,128)S(1)}, u32[]{:S(2)}, u32[]{:S(2)}) collective-permute-start(f32[8,256]{1,0:T(8,128)S(1)} %get-tuple-element.34.st0), channel_id=1, source_target_pairs={{32,0},{36,4},{40,8},{44,12},{48,16},{52,20},{56,24},{60,28},{64,3... | collective-permute-start | bytes 24584 | tf_op jit(solution)/shard_map/ppermute | solution.py:494
  89.3 2.0 %chain_walk.1 = bf16[8,64,128]{2,1,0:T(8,128)(2,1)} custom-call(bf16[208,128]{1,0:T(8,128)(2,1)S(1)} %collective-permute-done.21.refs_0_, bf16[208,128]{1,0:T(8,128)(2,1)S(1)} %collective-permute-done.22.refs_1_, bf16[208,128]{1,0:T(8,128)(2,1)S(1)} %collective-permute-done.23.refs_2_, bf16[8,208,128]{2,1,0:T(8,128)(2,1)S(1)} %all-to-all-done.blocks_ref.refs_3_), custom_call_target="tpu_custom_call" | custom-call | bytes 262144 | tf_op jit(solution)/shard_map/chain_walk/pallas_call | solution.py:475
  91.3 4.6 %all-to-all-start.1 = ((bf16[8,64,128]{2,1,0:T(8,128)(2,1)}), bf16[8,64,128]{2,1,0:T(8,128)(2,1)S(1)}, u32[]{:S(2)}, u32[]{:S(2)}) async-start(bf16[8,64,128]{2,1,0:T(8,128)(2,1)} %chain_walk.1), calls=%async_computation.1 | async-start | bytes 262144 | tf_op jit(solution)/shard_map/all_to_all | solution.py:476
  97.8 2.2 %att_cols.1 = (bf16[3,128,256]{2,1,0:T(8,128)(2,1)S(1)}, bf16[3,128,256]{2,1,0:T(8,128)(2,1)S(1)}) custom-call(bf16[2,256,256]{2,1,0:T(8,128)(2,1)S(1)} %get-tuple-element.29.kv0.kv_ref, bf16[256,256]{1,0:T(8,128)(2,1)S(1)} %copy-done.21, bf16[2,256,256]{2,1,0:T(8,128)(2,1)S(1)} %att_join_dout.1.qd_ref.qd0, ...), custom_call_target="tpu_custom_call" | custom-call | flops 3000000000 | bytes 786432 | tf_op jit(solution)/shard_map/att_cols/pallas_call | solution.py:500
  100.1 2.5 %all-to-all-done.1 = bf16[8,64,128]{2,1,0:T(8,128)(2,1)S(1)} async-done(((bf16[8,64,128]{2,1,0:T(8,128)(2,1)}), bf16[8,64,128]{2,1,0:T(8,128)(2,1)S(1)}, u32[]{:S(2)}, u32[]{:S(2)}) %all-to-all-start.1) | async-done | bytes 131104 | tf_op jit(solution)/shard_map/all_to_all | solution.py:476
  102.6 4.5 %gdn_post.1 = (bf16[128,512]{1,0:T(8,128)(2,1)}, bf16[128,512]{1,0:T(8,128)(2,1)}, bf16[128,512]{1,0:T(8,128)(2,1)}, f32[4,128]{1,0:T(4,128)}, f32[4,128]{1,0:T(4,128)}) custom-call(bf16[128,512]{1,0:T(8,128)(2,1)S(1)} %copy-done.11, bf16[128,512]{1,0:T(8,128)(2,1)S(1)} %copy-done.12, bf16[128,512]{1,0:T(8,128)(2,1)S(1)} %copy-done.13, ...), custom_call_target="tpu_custom_call" | custom-call | flops 5000000000 | bytes 794624 | tf_op jit(solution)/shard_map/gdn_post/pallas_call | solution.py:477
  (84 shorter events, 20.2 us)
Async XLA Ops:
  0.6 9.6 %collective-permute-start.1 = (bf16[128,512]{1,0:T(8,128)(2,1)}, bf16[128,512]{1,0:T(8,128)(2,1)S(1)}, u32[]{:S(2)}, u32[]{:S(2)}) collective-permute-start(bf16[128,512]{1,0:T(8,128)(2,1)} %d0.1), channel_id=1, source_target_pairs={{0,1},{1,2},{2,3},{3,0},{4,5},{5,6},{6,7},{7,4},{8,9},{9,10},{10,1... | collective-permute-start | bytes 393224 | tf_op jit(solution)/shard_map/ppermute | solution.py:439
  2.3 9.9 %collective-permute-start.2 = (bf16[128,512]{1,0:T(8,128)(2,1)}, bf16[128,512]{1,0:T(8,128)(2,1)S(1)}, u32[]{:S(2)}, u32[]{:S(2)}) collective-permute-start(bf16[128,512]{1,0:T(8,128)(2,1)} %d0.1), channel_id=1, source_target_pairs={{0,2},{1,3},{2,0},{3,1},{4,6},{5,7},{6,4},{7,5},{8,10},{9,11},{10,... | collective-permute-start | bytes 393224 | tf_op jit(solution)/shard_map/ppermute | solution.py:439
  5.2 7.8 %collective-permute-start.3 = (bf16[128,512]{1,0:T(8,128)(2,1)}, bf16[128,512]{1,0:T(8,128)(2,1)S(1)}, u32[]{:S(2)}, u32[]{:S(2)}) collective-permute-start(bf16[128,512]{1,0:T(8,128)(2,1)} %d0.1), channel_id=1, source_target_pairs={{0,3},{1,0},{2,1},{3,2},{4,7},{5,4},{6,5},{7,6},{8,11},{9,8},{10,9... | collective-permute-start | bytes 393224 | tf_op jit(solution)/shard_map/ppermute | solution.py:439
  9.4 24.1 %collective-permute-start.18 = (bf16[128,512]{1,0:T(8,128)(2,1)}, bf16[128,512]{1,0:T(8,128)(2,1)S(1)}, u32[]{:S(2)}, u32[]{:S(2)}) collective-permute-start(bf16[128,512]{1,0:T(8,128)(2,1)} %refs_0_.4), channel_id=1, source_target_pairs={{0,1},{1,2},{2,3},{3,0},{4,5},{5,6},{6,7},{7,4},{8,9},{9,10},{10,1... | collective-permute-start | bytes 393224 | tf_op jit(solution)/shard_map/ppermute | solution.py:439
  10.2 23.4 %collective-permute-start.19 = (bf16[128,512]{1,0:T(8,128)(2,1)}, bf16[128,512]{1,0:T(8,128)(2,1)S(1)}, u32[]{:S(2)}, u32[]{:S(2)}) collective-permute-start(bf16[128,512]{1,0:T(8,128)(2,1)} %refs_0_.4), channel_id=1, source_target_pairs={{0,2},{1,3},{2,0},{3,1},{4,6},{5,7},{6,4},{7,5},{8,10},{9,11},{10,... | collective-permute-start | bytes 393224 | tf_op jit(solution)/shard_map/ppermute | solution.py:439
  12.2 21.4 %collective-permute-start.20 = (bf16[128,512]{1,0:T(8,128)(2,1)}, bf16[128,512]{1,0:T(8,128)(2,1)S(1)}, u32[]{:S(2)}, u32[]{:S(2)}) collective-permute-start(bf16[128,512]{1,0:T(8,128)(2,1)} %refs_0_.4), channel_id=1, source_target_pairs={{0,3},{1,0},{2,1},{3,2},{4,7},{5,4},{6,5},{7,6},{8,11},{9,8},{10,9... | collective-permute-start | bytes 393224 | tf_op jit(solution)/shard_map/ppermute | solution.py:439
  16.3 8.3 %collective-permute-start.4 = (bf16[128,256]{1,0:T(8,128)(2,1)S(1)}, bf16[128,256]{1,0:T(8,128)(2,1)S(1)}, u32[]{:S(2)}, u32[]{:S(2)}) collective-permute-start(bf16[128,256]{1,0:T(8,128)(2,1)S(1)} %get-tuple-element.32), channel_id=1, source_target_pairs={{0,4},{4,0},{8,12},{12,8},{16,20},{20,16},{24,28},{28,24},{32,36},... | collective-permute-start | bytes 196616 | tf_op jit(solution)/shard_map/ppermute | solution.py:486
  16.5 15.1 %collective-permute-start.5 = (bf16[2,256,256]{2,1,0:T(8,128)(2,1)S(1)}, bf16[2,256,256]{2,1,0:T(8,128)(2,1)S(1)}, u32[]{:S(2)}, u32[]{:S(2)}) collective-permute-start(bf16[2,256,256]{2,1,0:T(8,128)(2,1)S(1)} %get-tuple-element.29.kv0.kv_ref), channel_id=1, source_target_pairs={{0,8},{4,12},{8,16},{12,20},{16,24},{20,28},{24,32},{28,36},{32,40... | collective-permute-start | bytes 786440 | tf_op jit(solution)/shard_map/ppermute | solution.py:452
  24.7 16.6 %collective-permute-start.9 = (bf16[2,256,256]{2,1,0:T(8,128)(2,1)S(1)}, bf16[2,256,256]{2,1,0:T(8,128)(2,1)S(1)}, u32[]{:S(2)}, u32[]{:S(2)}) collective-permute-start(bf16[2,256,256]{2,1,0:T(8,128)(2,1)S(1)} %att_join_dout.1.qd_ref.qd0), channel_id=1, source_target_pairs={{8,0},{12,4},{16,8},{20,12},{24,16},{28,20},{32,24},{36,28},{40,32... | collective-permute-start | bytes 786440 | tf_op jit(solution)/shard_map/ppermute | solution.py:489
  31.6 14.9 %collective-permute-start.6 = (bf16[2,256,256]{2,1,0:T(8,128)(2,1)S(1)}, bf16[2,256,256]{2,1,0:T(8,128)(2,1)S(1)}, u32[]{:S(2)}, u32[]{:S(2)}) collective-permute-start(bf16[2,256,256]{2,1,0:T(8,128)(2,1)S(1)} %collective-permute-done.5.kv1), channel_id=1, source_target_pairs={{0,8},{4,12},{8,16},{12,20},{16,24},{20,28},{24,32},{28,36},{32,40... | collective-permute-start | bytes 786440 | tf_op jit(solution)/shard_map/ppermute | solution.py:452
  35.4 29.2 %all-to-all-start = ((bf16[8,208,128]{2,1,0:T(8,128)(2,1)}), bf16[8,208,128]{2,1,0:T(8,128)(2,1)S(1)}, u32[]{:S(2)}, u32[]{:S(2)}) async-start(bf16[8,208,128]{2,1,0:T(8,128)(2,1)} %get-tuple-element.44), calls=%async_computation | async-start | bytes 851968 | tf_op jit(solution)/shard_map/all_to_all | solution.py:466
  41.3 15.7 %collective-permute-start.10 = (bf16[2,256,256]{2,1,0:T(8,128)(2,1)S(1)}, bf16[2,256,256]{2,1,0:T(8,128)(2,1)S(1)}, u32[]{:S(2)}, u32[]{:S(2)}) collective-permute-start(bf16[2,256,256]{2,1,0:T(8,128)(2,1)S(1)} %collective-permute-done.9.qd1), channel_id=1, source_target_pairs={{8,0},{12,4},{16,8},{20,12},{24,16},{28,20},{32,24},{36,28},{40,32... | collective-permute-start | bytes 786440 | tf_op jit(solution)/shard_map/ppermute | solution.py:489
  46.6 13.3 %collective-permute-start.7 = (bf16[2,256,256]{2,1,0:T(8,128)(2,1)S(1)}, bf16[2,256,256]{2,1,0:T(8,128)(2,1)S(1)}, u32[]{:S(2)}, u32[]{:S(2)}) collective-permute-start(bf16[2,256,256]{2,1,0:T(8,128)(2,1)S(1)} %collective-permute-done.6.kv2), channel_id=1, source_target_pairs={{0,8},{4,12},{8,16},{12,20},{16,24},{20,28},{24,32},{28,36},{32,40... | collective-permute-start | bytes 786440 | tf_op jit(solution)/shard_map/ppermute | solution.py:452
  57.0 15.4 %collective-permute-start.11 = (bf16[2,256,256]{2,1,0:T(8,128)(2,1)S(1)}, bf16[2,256,256]{2,1,0:T(8,128)(2,1)S(1)}, u32[]{:S(2)}, u32[]{:S(2)}) collective-permute-start(bf16[2,256,256]{2,1,0:T(8,128)(2,1)S(1)} %collective-permute-done.10.qd2), channel_id=1, source_target_pairs={{8,0},{12,4},{16,8},{20,12},{24,16},{28,20},{32,24},{36,28},{40,32... | collective-permute-start | bytes 786440 | tf_op jit(solution)/shard_map/ppermute | solution.py:489
  59.9 15.6 %collective-permute-start.8 = (bf16[2,256,256]{2,1,0:T(8,128)(2,1)S(1)}, bf16[2,256,256]{2,1,0:T(8,128)(2,1)S(1)}, u32[]{:S(2)}, u32[]{:S(2)}) collective-permute-start(bf16[2,256,256]{2,1,0:T(8,128)(2,1)S(1)} %collective-permute-done.7.kv3), channel_id=1, source_target_pairs={{0,8},{4,12},{8,16},{12,20},{16,24},{20,28},{24,32},{28,36},{32,40... | collective-permute-start | bytes 786440 | tf_op jit(solution)/shard_map/ppermute | solution.py:452
  65.7 15.8 %collective-permute-start.21 = (bf16[208,128]{1,0:T(8,128)(2,1)S(1)}, bf16[208,128]{1,0:T(8,128)(2,1)S(1)}, u32[]{:S(2)}, u32[]{:S(2)}) collective-permute-start(bf16[208,128]{1,0:T(8,128)(2,1)S(1)} %chain_fold.1), channel_id=1, source_target_pairs={{32,0},{36,4},{40,8},{44,12},{48,16},{52,20},{56,24},{60,28},{64,3... | collective-permute-start | bytes 159752 | tf_op jit(solution)/shard_map/ppermute | solution.py:469
  70.4 14.5 %collective-permute-start.22 = (bf16[208,128]{1,0:T(8,128)(2,1)S(1)}, bf16[208,128]{1,0:T(8,128)(2,1)S(1)}, u32[]{:S(2)}, u32[]{:S(2)}) collective-permute-start(bf16[208,128]{1,0:T(8,128)(2,1)S(1)} %chain_fold.1), channel_id=1, source_target_pairs={{64,0},{68,4},{72,8},{76,12},{80,16},{84,20},{88,24},{92,28},{96,3... | collective-permute-start | bytes 159752 | tf_op jit(solution)/shard_map/ppermute | solution.py:469
  71.7 15.7 %collective-permute-start.23 = (bf16[208,128]{1,0:T(8,128)(2,1)S(1)}, bf16[208,128]{1,0:T(8,128)(2,1)S(1)}, u32[]{:S(2)}, u32[]{:S(2)}) collective-permute-start(bf16[208,128]{1,0:T(8,128)(2,1)S(1)} %chain_fold.1), channel_id=1, source_target_pairs={{96,0},{100,4},{104,8},{108,12},{112,16},{116,20},{120,24},{124,28... | collective-permute-start | bytes 159752 | tf_op jit(solution)/shard_map/ppermute | solution.py:469
  72.4 23.4 %collective-permute-start.12 = (bf16[2,256,256]{2,1,0:T(8,128)(2,1)S(1)}, bf16[2,256,256]{2,1,0:T(8,128)(2,1)S(1)}, u32[]{:S(2)}, u32[]{:S(2)}) collective-permute-start(bf16[2,256,256]{2,1,0:T(8,128)(2,1)S(1)} %collective-permute-done.11.qd3), channel_id=1, source_target_pairs={{8,0},{12,4},{16,8},{20,12},{24,16},{28,20},{32,24},{36,28},{40,32... | collective-permute-start | bytes 786440 | tf_op jit(solution)/shard_map/ppermute | solution.py:489
  77.6 18.3 %collective-permute-start.13 = (f32[8,256]{1,0:T(8,128)S(1)}, f32[8,256]{1,0:T(8,128)S(1)}, u32[]{:S(2)}, u32[]{:S(2)}) collective-permute-start(f32[8,256]{1,0:T(8,128)S(1)} %get-tuple-element.34.st0), channel_id=1, source_target_pairs={{8,0},{12,4},{16,8},{20,12},{24,16},{28,20},{32,24},{36,28},{40,32... | collective-permute-start | bytes 24584 | tf_op jit(solution)/shard_map/ppermute | solution.py:494
  81.5 14.3 %collective-permute-start.14 = (f32[8,256]{1,0:T(8,128)S(1)}, f32[8,256]{1,0:T(8,128)S(1)}, u32[]{:S(2)}, u32[]{:S(2)}) collective-permute-start(f32[8,256]{1,0:T(8,128)S(1)} %get-tuple-element.34.st0), channel_id=1, source_target_pairs={{16,0},{20,4},{24,8},{28,12},{32,16},{36,20},{40,24},{44,28},{48,3... | collective-permute-start | bytes 24584 | tf_op jit(solution)/shard_map/ppermute | solution.py:494
  84.9 10.9 %collective-permute-start.15 = (f32[8,256]{1,0:T(8,128)S(1)}, f32[8,256]{1,0:T(8,128)S(1)}, u32[]{:S(2)}, u32[]{:S(2)}) collective-permute-start(f32[8,256]{1,0:T(8,128)S(1)} %get-tuple-element.34.st0), channel_id=1, source_target_pairs={{24,0},{28,4},{32,8},{36,12},{40,16},{44,20},{48,24},{52,28},{56,3... | collective-permute-start | bytes 24584 | tf_op jit(solution)/shard_map/ppermute | solution.py:494
  87.4 9.5 %collective-permute-start.16 = (f32[8,256]{1,0:T(8,128)S(1)}, f32[8,256]{1,0:T(8,128)S(1)}, u32[]{:S(2)}, u32[]{:S(2)}) collective-permute-start(f32[8,256]{1,0:T(8,128)S(1)} %get-tuple-element.34.st0), channel_id=1, source_target_pairs={{32,0},{36,4},{40,8},{44,12},{48,16},{52,20},{56,24},{60,28},{64,3... | collective-permute-start | bytes 24584 | tf_op jit(solution)/shard_map/ppermute | solution.py:494
  91.3 11.3 %all-to-all-start.1 = ((bf16[8,64,128]{2,1,0:T(8,128)(2,1)}), bf16[8,64,128]{2,1,0:T(8,128)(2,1)S(1)}, u32[]{:S(2)}, u32[]{:S(2)}) async-start(bf16[8,64,128]{2,1,0:T(8,128)(2,1)} %chain_walk.1), calls=%async_computation.1 | async-start | bytes 262144 | tf_op jit(solution)/shard_map/all_to_all | solution.py:476
  (24 other events, 167.3 us)

commit v3 on v2

--- a/solution.py
+++ b/solution.py
@@ -408,7 +408,7 @@
         body,
         out_shape=shapes if len(shapes) > 1 else shapes[0],
         scratch_shapes=list(scratch),
-        compiler_params=pltpu.CompilerParams(vmem_limit_bytes=48 * 1024 * 1024),
+        compiler_params=pltpu.CompilerParams(vmem_limit_bytes=24 * 1024 * 1024),
         cost_estimate=pl.CostEstimate(flops=flops, bytes_accessed=2 * nbytes, transcendentals=0),
         name=name,
     )
@@ -495,8 +495,8 @@
             stats, "seq",
             [(i, i - 2 * s) for i in range(seq_count) if i % per_doc >= 2 * s],
         )
-        for s in range(1, RING + 1)
-    ]
+        for s in range(RING, 0, -1)
+    ][::-1]
     keep, send = kernel(
         att_cols_body, [((3, toks, PAIR), BF16)] * 2, "att_cols", flops=3 * 10**9,
         scratch=[pltpu.VMEM((3, PAIR, PAIR), BF16)],

time: 109 us -> 109 us (level)
  no operation moved by 1% of the time
where the time goes in v3:
time: 109 us; the launch traced here: 108 us
  starting transfers between devices  68.4 us (63%)
  Pallas kernels  18.7 us (17%)
  waiting for transfers between devices  12.8 us (12%)
  local copies, waits for them, and re-layouts  6.89 us (6%)
  between operations  1.13 us (1%)
    ppermute x4, starting transfers between devices, shards(): qd.append(lax.ppermute(qd[-1], 'seq', back))  17.4 us
    ppermute x4, starting transfers between devices, shards(): kv.append(lax.ppermute(kv[-1], 'seq', forth))  12.5 us
    ppermute x4, starting transfers between devices, shards(): lax.ppermute(stats, 'seq', [(i, i - 2 * s) for i in range(seq_count) if i...  11.7 us
    ppermute x6, starting transfers between devices, gathered(): lax.ppermute(value, 'head', [(i, (i + s) % head_count) for i in range(hea...  9.44 us
    ppermute x4, waiting for transfers between devices, shards(): qd.append(lax.ppermute(qd[-1], 'seq', back))  8.47 us
    unnamed x44, local copies, waits for them, and re-layouts  6.89 us
    ppermute x3, starting transfers between devices, shards(): lax.ppermute(folded, 'seq', [(i, i - SEG * s) for i in range(seq_count) i...  6.68 us
    all_to_all x1, starting transfers between devices, shards(): blocks = lax.all_to_all(payload, 'seq', 0, 0, axis_index_groups=quads)  5.84 us
  transfers between devices with their start and end apart: 26, of which 4 were waited for; matrix products, arithmetic and copies ran while one was open for 0% of the time, Pallas kernels for 17%

profile of v3, /device:TPU:6, one launch (start us, length us, event | category | flops | bytes accessed | tf_op | source)
XLA Modules:
  0.0 108.0 jit_solution(17907607929797285520)
XLA Ops:
  2.3 2.9 %collective-permute-start.2 = (bf16[128,512]{1,0:T(8,128)(2,1)}, bf16[128,512]{1,0:T(8,128)(2,1)S(1)}, u32[]{:S(2)}, u32[]{:S(2)}) collective-permute-start(bf16[128,512]{1,0:T(8,128)(2,1)} %d0.1), channel_id=1, source_target_pairs={{0,2},{1,3},{2,0},{3,1},{4,6},{5,7},{6,4},{7,5},{8,10},{9,11},{10,... | collective-permute-start | bytes 393224 | tf_op jit(solution)/shard_map/ppermute | solution.py:439
  10.2 2.0 %collective-permute-start.19 = (bf16[128,512]{1,0:T(8,128)(2,1)}, bf16[128,512]{1,0:T(8,128)(2,1)S(1)}, u32[]{:S(2)}, u32[]{:S(2)}) collective-permute-start(bf16[128,512]{1,0:T(8,128)(2,1)} %refs_0_.4), channel_id=1, source_target_pairs={{0,2},{1,3},{2,0},{3,1},{4,6},{5,7},{6,4},{7,5},{8,10},{9,11},{10,... | collective-permute-start | bytes 393224 | tf_op jit(solution)/shard_map/ppermute | solution.py:439
  16.5 4.0 %collective-permute-start.5 = (bf16[2,256,256]{2,1,0:T(8,128)(2,1)S(1)}, bf16[2,256,256]{2,1,0:T(8,128)(2,1)S(1)}, u32[]{:S(2)}, u32[]{:S(2)}) collective-permute-start(bf16[2,256,256]{2,1,0:T(8,128)(2,1)S(1)} %get-tuple-element.29.kv0.kv_ref), channel_id=1, source_target_pairs={{0,8},{4,12},{8,16},{12,20},{16,24},{20,28},{24,32},{28,36},{32,40... | collective-permute-start | bytes 786440 | tf_op jit(solution)/shard_map/ppermute | solution.py:452
  20.5 3.4 %gdn_pre.1 = (f32[4,128,128]{2,1,0:T(8,128)S(1)}, f32[4,128,128]{2,1,0:T(8,128)S(1)}, bf16[4,144,128]{2,1,0:T(8,128)(2,1)S(1)}) custom-call(bf16[128,512]{1,0:T(8,128)(2,1)S(1)} %copy-done.11, bf16[128,512]{1,0:T(8,128)(2,1)S(1)} %copy-done.12, f32[4,128]{1,0:T(4,128)S(1)} %copy-done.14, f32[4,128]{1,0:T(4,128)S(1)} %copy-done.15), custom_call_target="tpu_custom_call" | custom-call | flops 3000000000 | bytes 1343488 | tf_op jit(solution)/shard_map/gdn_pre/pallas_call | solution.py:454
  24.7 6.1 %collective-permute-start.9 = (bf16[2,256,256]{2,1,0:T(8,128)(2,1)S(1)}, bf16[2,256,256]{2,1,0:T(8,128)(2,1)S(1)}, u32[]{:S(2)}, u32[]{:S(2)}) collective-permute-start(bf16[2,256,256]{2,1,0:T(8,128)(2,1)S(1)} %att_join_dout.1.qd_ref.qd0), channel_id=1, source_target_pairs={{8,0},{12,4},{16,8},{20,12},{24,16},{28,20},{32,24},{36,28},{40,32... | collective-permute-start | bytes 786440 | tf_op jit(solution)/shard_map/ppermute | solution.py:489
  31.6 1.9 %collective-permute-start.6 = (bf16[2,256,256]{2,1,0:T(8,128)(2,1)S(1)}, bf16[2,256,256]{2,1,0:T(8,128)(2,1)S(1)}, u32[]{:S(2)}, u32[]{:S(2)}) collective-permute-start(bf16[2,256,256]{2,1,0:T(8,128)(2,1)S(1)} %collective-permute-done.5.kv1), channel_id=1, source_target_pairs={{0,8},{4,12},{8,16},{12,20},{16,24},{20,28},{24,32},{28,36},{32,40... | collective-permute-start | bytes 786440 | tf_op jit(solution)/shard_map/ppermute | solution.py:452
  35.4 5.8 %all-to-all-start = ((bf16[8,208,128]{2,1,0:T(8,128)(2,1)}), bf16[8,208,128]{2,1,0:T(8,128)(2,1)S(1)}, u32[]{:S(2)}, u32[]{:S(2)}) async-start(bf16[8,208,128]{2,1,0:T(8,128)(2,1)} %get-tuple-element.44), calls=%async_computation | async-start | bytes 851968 | tf_op jit(solution)/shard_map/all_to_all | solution.py:466
  41.3 5.3 %collective-permute-start.10 = (bf16[2,256,256]{2,1,0:T(8,128)(2,1)S(1)}, bf16[2,256,256]{2,1,0:T(8,128)(2,1)S(1)}, u32[]{:S(2)}, u32[]{:S(2)}) collective-permute-start(bf16[2,256,256]{2,1,0:T(8,128)(2,1)S(1)} %collective-permute-done.9.qd1), channel_id=1, source_target_pairs={{8,0},{12,4},{16,8},{20,12},{24,16},{28,20},{32,24},{36,28},{40,32... | collective-permute-start | bytes 786440 | tf_op jit(solution)/shard_map/ppermute | solution.py:489
  46.6 1.9 %collective-permute-start.7 = (bf16[2,256,256]{2,1,0:T(8,128)(2,1)S(1)}, bf16[2,256,256]{2,1,0:T(8,128)(2,1)S(1)}, u32[]{:S(2)}, u32[]{:S(2)}) collective-permute-start(bf16[2,256,256]{2,1,0:T(8,128)(2,1)S(1)} %collective-permute-done.6.kv2), channel_id=1, source_target_pairs={{0,8},{4,12},{8,16},{12,20},{16,24},{20,28},{24,32},{28,36},{32,40... | collective-permute-start | bytes 786440 | tf_op jit(solution)/shard_map/ppermute | solution.py:452
  48.5 8.5 %collective-permute-done.10.qd2 = bf16[2,256,256]{2,1,0:T(8,128)(2,1)S(1)} collective-permute-done((bf16[2,256,256]{2,1,0:T(8,128)(2,1)S(1)}, bf16[2,256,256]{2,1,0:T(8,128)(2,1)S(1)}, u32[]{:S(2)}, u32[]{:S(2)}) %collective-permute-start.10) | collective-permute-done | bytes 262176 | tf_op jit(solution)/shard_map/ppermute | solution.py:489
  57.0 2.9 %collective-permute-start.11 = (bf16[2,256,256]{2,1,0:T(8,128)(2,1)S(1)}, bf16[2,256,256]{2,1,0:T(8,128)(2,1)S(1)}, u32[]{:S(2)}, u32[]{:S(2)}) collective-permute-start(bf16[2,256,256]{2,1,0:T(8,128)(2,1)S(1)} %collective-permute-done.10.qd2), channel_id=1, source_target_pairs={{8,0},{12,4},{16,8},{20,12},{24,16},{28,20},{32,24},{36,28},{40,32... | collective-permute-start | bytes 786440 | tf_op jit(solution)/shard_map/ppermute | solution.py:489
  59.9 4.7 %collective-permute-start.8 = (bf16[2,256,256]{2,1,0:T(8,128)(2,1)S(1)}, bf16[2,256,256]{2,1,0:T(8,128)(2,1)S(1)}, u32[]{:S(2)}, u32[]{:S(2)}) collective-permute-start(bf16[2,256,256]{2,1,0:T(8,128)(2,1)S(1)} %collective-permute-done.7.kv3), channel_id=1, source_target_pairs={{0,8},{4,12},{8,16},{12,20},{16,24},{20,28},{24,32},{28,36},{32,40... | collective-permute-start | bytes 786440 | tf_op jit(solution)/shard_map/ppermute | solution.py:452
  65.7 4.7 %collective-permute-start.21 = (bf16[208,128]{1,0:T(8,128)(2,1)S(1)}, bf16[208,128]{1,0:T(8,128)(2,1)S(1)}, u32[]{:S(2)}, u32[]{:S(2)}) collective-permute-start(bf16[208,128]{1,0:T(8,128)(2,1)S(1)} %chain_fold.1), channel_id=1, source_target_pairs={{32,0},{36,4},{40,8},{44,12},{48,16},{52,20},{56,24},{60,28},{64,3... | collective-permute-start | bytes 159752 | tf_op jit(solution)/shard_map/ppermute | solution.py:469
  72.4 3.1 %collective-permute-start.12 = (bf16[2,256,256]{2,1,0:T(8,128)(2,1)S(1)}, bf16[2,256,256]{2,1,0:T(8,128)(2,1)S(1)}, u32[]{:S(2)}, u32[]{:S(2)}) collective-permute-start(bf16[2,256,256]{2,1,0:T(8,128)(2,1)S(1)} %collective-permute-done.11.qd3), channel_id=1, source_target_pairs={{8,0},{12,4},{16,8},{20,12},{24,16},{28,20},{32,24},{36,28},{40,32... | collective-permute-start | bytes 786440 | tf_op jit(solution)/shard_map/ppermute | solution.py:489
  75.5 2.0 %att_rows.1 = (bf16[256,256]{1,0:T(8,128)(2,1)S(1)}, f32[8,256]{1,0:T(8,128)S(1)}) custom-call(bf16[2,256,256]{2,1,0:T(8,128)(2,1)S(1)} %att_join_dout.1.qd_ref.qd0, bf16[2,256,256]{2,1,0:T(8,128)(2,1)S(1)} %get-tuple-element.29.kv0.kv_ref, bf16[2,256,256]{2,1,0:T(8,128)(2,1)S(1)} %collective-permute-done.5.kv1, ...), custom_call_target="tpu_custom_call" | custom-call | flops 3000000000 | bytes 278528 | tf_op jit(solution)/shard_map/att_rows/pallas_call | solution.py:490
  77.6 3.9 %collective-permute-start.13 = (f32[8,256]{1,0:T(8,128)S(1)}, f32[8,256]{1,0:T(8,128)S(1)}, u32[]{:S(2)}, u32[]{:S(2)}) collective-permute-start(f32[8,256]{1,0:T(8,128)S(1)} %get-tuple-element.34.st0), channel_id=1, source_target_pairs={{8,0},{12,4},{16,8},{20,12},{24,16},{28,20},{32,24},{36,28},{40,32... | collective-permute-start | bytes 24584 | tf_op jit(solution)/shard_map/ppermute | solution.py:494
  81.5 3.4 %collective-permute-start.14 = (f32[8,256]{1,0:T(8,128)S(1)}, f32[8,256]{1,0:T(8,128)S(1)}, u32[]{:S(2)}, u32[]{:S(2)}) collective-permute-start(f32[8,256]{1,0:T(8,128)S(1)} %get-tuple-element.34.st0), channel_id=1, source_target_pairs={{16,0},{20,4},{24,8},{28,12},{32,16},{36,20},{40,24},{44,28},{48,3... | collective-permute-start | bytes 24584 | tf_op jit(solution)/shard_map/ppermute | solution.py:494
  84.9 2.5 %collective-permute-start.15 = (f32[8,256]{1,0:T(8,128)S(1)}, f32[8,256]{1,0:T(8,128)S(1)}, u32[]{:S(2)}, u32[]{:S(2)}) collective-permute-start(f32[8,256]{1,0:T(8,128)S(1)} %get-tuple-element.34.st0), channel_id=1, source_target_pairs={{24,0},{28,4},{32,8},{36,12},{40,16},{44,20},{48,24},{52,28},{56,3... | collective-permute-start | bytes 24584 | tf_op jit(solution)/shard_map/ppermute | solution.py:494
  87.4 1.9 %collective-permute-start.16 = (f32[8,256]{1,0:T(8,128)S(1)}, f32[8,256]{1,0:T(8,128)S(1)}, u32[]{:S(2)}, u32[]{:S(2)}) collective-permute-start(f32[8,256]{1,0:T(8,128)S(1)} %get-tuple-element.34.st0), channel_id=1, source_target_pairs={{32,0},{36,4},{40,8},{44,12},{48,16},{52,20},{56,24},{60,28},{64,3... | collective-permute-start | bytes 24584 | tf_op jit(solution)/shard_map/ppermute | solution.py:494
  89.3 2.0 %chain_walk.1 = bf16[8,64,128]{2,1,0:T(8,128)(2,1)} custom-call(bf16[208,128]{1,0:T(8,128)(2,1)S(1)} %collective-permute-done.21.refs_0_, bf16[208,128]{1,0:T(8,128)(2,1)S(1)} %collective-permute-done.22.refs_1_, bf16[208,128]{1,0:T(8,128)(2,1)S(1)} %collective-permute-done.23.refs_2_, bf16[8,208,128]{2,1,0:T(8,128)(2,1)S(1)} %all-to-all-done.blocks_ref.refs_3_), custom_call_target="tpu_custom_call" | custom-call | bytes 262144 | tf_op jit(solution)/shard_map/chain_walk/pallas_call | solution.py:475
  91.3 4.6 %all-to-all-start.1 = ((bf16[8,64,128]{2,1,0:T(8,128)(2,1)}), bf16[8,64,128]{2,1,0:T(8,128)(2,1)S(1)}, u32[]{:S(2)}, u32[]{:S(2)}) async-start(bf16[8,64,128]{2,1,0:T(8,128)(2,1)} %chain_walk.1), calls=%async_computation.1 | async-start | bytes 262144 | tf_op jit(solution)/shard_map/all_to_all | solution.py:476
  97.8 2.2 %att_cols.1 = (bf16[3,128,256]{2,1,0:T(8,128)(2,1)S(1)}, bf16[3,128,256]{2,1,0:T(8,128)(2,1)S(1)}) custom-call(bf16[2,256,256]{2,1,0:T(8,128)(2,1)S(1)} %get-tuple-element.29.kv0.kv_ref, bf16[256,256]{1,0:T(8,128)(2,1)S(1)} %copy-done.21, bf16[2,256,256]{2,1,0:T(8,128)(2,1)S(1)} %att_join_dout.1.qd_ref.qd0, ...), custom_call_target="tpu_custom_call" | custom-call | flops 3000000000 | bytes 786432 | tf_op jit(solution)/shard_map/att_cols/pallas_call | solution.py:500
  100.1 2.5 %all-to-all-done.1 = bf16[8,64,128]{2,1,0:T(8,128)(2,1)S(1)} async-done(((bf16[8,64,128]{2,1,0:T(8,128)(2,1)}), bf16[8,64,128]{2,1,0:T(8,128)(2,1)S(1)}, u32[]{:S(2)}, u32[]{:S(2)}) %all-to-all-start.1) | async-done | bytes 131104 | tf_op jit(solution)/shard_map/all_to_all | solution.py:476
  102.6 4.5 %gdn_post.1 = (bf16[128,512]{1,0:T(8,128)(2,1)}, bf16[128,512]{1,0:T(8,128)(2,1)}, bf16[128,512]{1,0:T(8,128)(2,1)}, f32[4,128]{1,0:T(4,128)}, f32[4,128]{1,0:T(4,128)}) custom-call(bf16[128,512]{1,0:T(8,128)(2,1)S(1)} %copy-done.11, bf16[128,512]{1,0:T(8,128)(2,1)S(1)} %copy-done.12, bf16[128,512]{1,0:T(8,128)(2,1)S(1)} %copy-done.13, ...), custom_call_target="tpu_custom_call" | custom-call | flops 5000000000 | bytes 794624 | tf_op jit(solution)/shard_map/gdn_post/pallas_call | solution.py:477
  (84 shorter events, 20.2 us)
Async XLA Ops:
  0.6 9.6 %collective-permute-start.1 = (bf16[128,512]{1,0:T(8,128)(2,1)}, bf16[128,512]{1,0:T(8,128)(2,1)S(1)}, u32[]{:S(2)}, u32[]{:S(2)}) collective-permute-start(bf16[128,512]{1,0:T(8,128)(2,1)} %d0.1), channel_id=1, source_target_pairs={{0,1},{1,2},{2,3},{3,0},{4,5},{5,6},{6,7},{7,4},{8,9},{9,10},{10,1... | collective-permute-start | bytes 393224 | tf_op jit(solution)/shard_map/ppermute | solution.py:439
  2.3 9.9 %collective-permute-start.2 = (bf16[128,512]{1,0:T(8,128)(2,1)}, bf16[128,512]{1,0:T(8,128)(2,1)S(1)}, u32[]{:S(2)}, u32[]{:S(2)}) collective-permute-start(bf16[128,512]{1,0:T(8,128)(2,1)} %d0.1), channel_id=1, source_target_pairs={{0,2},{1,3},{2,0},{3,1},{4,6},{5,7},{6,4},{7,5},{8,10},{9,11},{10,... | collective-permute-start | bytes 393224 | tf_op jit(solution)/shard_map/ppermute | solution.py:439
  5.2 7.8 %collective-permute-start.3 = (bf16[128,512]{1,0:T(8,128)(2,1)}, bf16[128,512]{1,0:T(8,128)(2,1)S(1)}, u32[]{:S(2)}, u32[]{:S(2)}) collective-permute-start(bf16[128,512]{1,0:T(8,128)(2,1)} %d0.1), channel_id=1, source_target_pairs={{0,3},{1,0},{2,1},{3,2},{4,7},{5,4},{6,5},{7,6},{8,11},{9,8},{10,9... | collective-permute-start | bytes 393224 | tf_op jit(solution)/shard_map/ppermute | solution.py:439
  9.4 24.1 %collective-permute-start.18 = (bf16[128,512]{1,0:T(8,128)(2,1)}, bf16[128,512]{1,0:T(8,128)(2,1)S(1)}, u32[]{:S(2)}, u32[]{:S(2)}) collective-permute-start(bf16[128,512]{1,0:T(8,128)(2,1)} %refs_0_.4), channel_id=1, source_target_pairs={{0,1},{1,2},{2,3},{3,0},{4,5},{5,6},{6,7},{7,4},{8,9},{9,10},{10,1... | collective-permute-start | bytes 393224 | tf_op jit(solution)/shard_map/ppermute | solution.py:439
  10.2 23.4 %collective-permute-start.19 = (bf16[128,512]{1,0:T(8,128)(2,1)}, bf16[128,512]{1,0:T(8,128)(2,1)S(1)}, u32[]{:S(2)}, u32[]{:S(2)}) collective-permute-start(bf16[128,512]{1,0:T(8,128)(2,1)} %refs_0_.4), channel_id=1, source_target_pairs={{0,2},{1,3},{2,0},{3,1},{4,6},{5,7},{6,4},{7,5},{8,10},{9,11},{10,... | collective-permute-start | bytes 393224 | tf_op jit(solution)/shard_map/ppermute | solution.py:439
  12.2 21.4 %collective-permute-start.20 = (bf16[128,512]{1,0:T(8,128)(2,1)}, bf16[128,512]{1,0:T(8,128)(2,1)S(1)}, u32[]{:S(2)}, u32[]{:S(2)}) collective-permute-start(bf16[128,512]{1,0:T(8,128)(2,1)} %refs_0_.4), channel_id=1, source_target_pairs={{0,3},{1,0},{2,1},{3,2},{4,7},{5,4},{6,5},{7,6},{8,11},{9,8},{10,9... | collective-permute-start | bytes 393224 | tf_op jit(solution)/shard_map/ppermute | solution.py:439
  16.3 8.3 %collective-permute-start.4 = (bf16[128,256]{1,0:T(8,128)(2,1)S(1)}, bf16[128,256]{1,0:T(8,128)(2,1)S(1)}, u32[]{:S(2)}, u32[]{:S(2)}) collective-permute-start(bf16[128,256]{1,0:T(8,128)(2,1)S(1)} %get-tuple-element.32), channel_id=1, source_target_pairs={{0,4},{4,0},{8,12},{12,8},{16,20},{20,16},{24,28},{28,24},{32,36},... | collective-permute-start | bytes 196616 | tf_op jit(solution)/shard_map/ppermute | solution.py:486
  16.5 15.1 %collective-permute-start.5 = (bf16[2,256,256]{2,1,0:T(8,128)(2,1)S(1)}, bf16[2,256,256]{2,1,0:T(8,128)(2,1)S(1)}, u32[]{:S(2)}, u32[]{:S(2)}) collective-permute-start(bf16[2,256,256]{2,1,0:T(8,128)(2,1)S(1)} %get-tuple-element.29.kv0.kv_ref), channel_id=1, source_target_pairs={{0,8},{4,12},{8,16},{12,20},{16,24},{20,28},{24,32},{28,36},{32,40... | collective-permute-start | bytes 786440 | tf_op jit(solution)/shard_map/ppermute | solution.py:452
  24.7 16.6 %collective-permute-start.9 = (bf16[2,256,256]{2,1,0:T(8,128)(2,1)S(1)}, bf16[2,256,256]{2,1,0:T(8,128)(2,1)S(1)}, u32[]{:S(2)}, u32[]{:S(2)}) collective-permute-start(bf16[2,256,256]{2,1,0:T(8,128)(2,1)S(1)} %att_join_dout.1.qd_ref.qd0), channel_id=1, source_target_pairs={{8,0},{12,4},{16,8},{20,12},{24,16},{28,20},{32,24},{36,28},{40,32... | collective-permute-start | bytes 786440 | tf_op jit(solution)/shard_map/ppermute | solution.py:489
  31.6 14.9 %collective-permute-start.6 = (bf16[2,256,256]{2,1,0:T(8,128)(2,1)S(1)}, bf16[2,256,256]{2,1,0:T(8,128)(2,1)S(1)}, u32[]{:S(2)}, u32[]{:S(2)}) collective-permute-start(bf16[2,256,256]{2,1,0:T(8,128)(2,1)S(1)} %collective-permute-done.5.kv1), channel_id=1, source_target_pairs={{0,8},{4,12},{8,16},{12,20},{16,24},{20,28},{24,32},{28,36},{32,40... | collective-permute-start | bytes 786440 | tf_op jit(solution)/shard_map/ppermute | solution.py:452
  35.4 29.2 %all-to-all-start = ((bf16[8,208,128]{2,1,0:T(8,128)(2,1)}), bf16[8,208,128]{2,1,0:T(8,128)(2,1)S(1)}, u32[]{:S(2)}, u32[]{:S(2)}) async-start(bf16[8,208,128]{2,1,0:T(8,128)(2,1)} %get-tuple-element.44), calls=%async_computation | async-start | bytes 851968 | tf_op jit(solution)/shard_map/all_to_all | solution.py:466
  41.3 15.7 %collective-permute-start.10 = (bf16[2,256,256]{2,1,0:T(8,128)(2,1)S(1)}, bf16[2,256,256]{2,1,0:T(8,128)(2,1)S(1)}, u32[]{:S(2)}, u32[]{:S(2)}) collective-permute-start(bf16[2,256,256]{2,1,0:T(8,128)(2,1)S(1)} %collective-permute-done.9.qd1), channel_id=1, source_target_pairs={{8,0},{12,4},{16,8},{20,12},{24,16},{28,20},{32,24},{36,28},{40,32... | collective-permute-start | bytes 786440 | tf_op jit(solution)/shard_map/ppermute | solution.py:489
  46.6 13.3 %collective-permute-start.7 = (bf16[2,256,256]{2,1,0:T(8,128)(2,1)S(1)}, bf16[2,256,256]{2,1,0:T(8,128)(2,1)S(1)}, u32[]{:S(2)}, u32[]{:S(2)}) collective-permute-start(bf16[2,256,256]{2,1,0:T(8,128)(2,1)S(1)} %collective-permute-done.6.kv2), channel_id=1, source_target_pairs={{0,8},{4,12},{8,16},{12,20},{16,24},{20,28},{24,32},{28,36},{32,40... | collective-permute-start | bytes 786440 | tf_op jit(solution)/shard_map/ppermute | solution.py:452
  57.0 15.4 %collective-permute-start.11 = (bf16[2,256,256]{2,1,0:T(8,128)(2,1)S(1)}, bf16[2,256,256]{2,1,0:T(8,128)(2,1)S(1)}, u32[]{:S(2)}, u32[]{:S(2)}) collective-permute-start(bf16[2,256,256]{2,1,0:T(8,128)(2,1)S(1)} %collective-permute-done.10.qd2), channel_id=1, source_target_pairs={{8,0},{12,4},{16,8},{20,12},{24,16},{28,20},{32,24},{36,28},{40,32... | collective-permute-start | bytes 786440 | tf_op jit(solution)/shard_map/ppermute | solution.py:489
  59.9 15.6 %collective-permute-start.8 = (bf16[2,256,256]{2,1,0:T(8,128)(2,1)S(1)}, bf16[2,256,256]{2,1,0:T(8,128)(2,1)S(1)}, u32[]{:S(2)}, u32[]{:S(2)}) collective-permute-start(bf16[2,256,256]{2,1,0:T(8,128)(2,1)S(1)} %collective-permute-done.7.kv3), channel_id=1, source_target_pairs={{0,8},{4,12},{8,16},{12,20},{16,24},{20,28},{24,32},{28,36},{32,40... | collective-permute-start | bytes 786440 | tf_op jit(solution)/shard_map/ppermute | solution.py:452
  65.7 15.8 %collective-permute-start.21 = (bf16[208,128]{1,0:T(8,128)(2,1)S(1)}, bf16[208,128]{1,0:T(8,128)(2,1)S(1)}, u32[]{:S(2)}, u32[]{:S(2)}) collective-permute-start(bf16[208,128]{1,0:T(8,128)(2,1)S(1)} %chain_fold.1), channel_id=1, source_target_pairs={{32,0},{36,4},{40,8},{44,12},{48,16},{52,20},{56,24},{60,28},{64,3... | collective-permute-start | bytes 159752 | tf_op jit(solution)/shard_map/ppermute | solution.py:469
  70.4 14.5 %collective-permute-start.22 = (bf16[208,128]{1,0:T(8,128)(2,1)S(1)}, bf16[208,128]{1,0:T(8,128)(2,1)S(1)}, u32[]{:S(2)}, u32[]{:S(2)}) collective-permute-start(bf16[208,128]{1,0:T(8,128)(2,1)S(1)} %chain_fold.1), channel_id=1, source_target_pairs={{64,0},{68,4},{72,8},{76,12},{80,16},{84,20},{88,24},{92,28},{96,3... | collective-permute-start | bytes 159752 | tf_op jit(solution)/shard_map/ppermute | solution.py:469
  71.7 15.7 %collective-permute-start.23 = (bf16[208,128]{1,0:T(8,128)(2,1)S(1)}, bf16[208,128]{1,0:T(8,128)(2,1)S(1)}, u32[]{:S(2)}, u32[]{:S(2)}) collective-permute-start(bf16[208,128]{1,0:T(8,128)(2,1)S(1)} %chain_fold.1), channel_id=1, source_target_pairs={{96,0},{100,4},{104,8},{108,12},{112,16},{116,20},{120,24},{124,28... | collective-permute-start | bytes 159752 | tf_op jit(solution)/shard_map/ppermute | solution.py:469
  72.4 23.4 %collective-permute-start.12 = (bf16[2,256,256]{2,1,0:T(8,128)(2,1)S(1)}, bf16[2,256,256]{2,1,0:T(8,128)(2,1)S(1)}, u32[]{:S(2)}, u32[]{:S(2)}) collective-permute-start(bf16[2,256,256]{2,1,0:T(8,128)(2,1)S(1)} %collective-permute-done.11.qd3), channel_id=1, source_target_pairs={{8,0},{12,4},{16,8},{20,12},{24,16},{28,20},{32,24},{36,28},{40,32... | collective-permute-start | bytes 786440 | tf_op jit(solution)/shard_map/ppermute | solution.py:489
  77.6 18.3 %collective-permute-start.13 = (f32[8,256]{1,0:T(8,128)S(1)}, f32[8,256]{1,0:T(8,128)S(1)}, u32[]{:S(2)}, u32[]{:S(2)}) collective-permute-start(f32[8,256]{1,0:T(8,128)S(1)} %get-tuple-element.34.st0), channel_id=1, source_target_pairs={{8,0},{12,4},{16,8},{20,12},{24,16},{28,20},{32,24},{36,28},{40,32... | collective-permute-start | bytes 24584 | tf_op jit(solution)/shard_map/ppermute | solution.py:494
  81.5 14.3 %collective-permute-start.14 = (f32[8,256]{1,0:T(8,128)S(1)}, f32[8,256]{1,0:T(8,128)S(1)}, u32[]{:S(2)}, u32[]{:S(2)}) collective-permute-start(f32[8,256]{1,0:T(8,128)S(1)} %get-tuple-element.34.st0), channel_id=1, source_target_pairs={{16,0},{20,4},{24,8},{28,12},{32,16},{36,20},{40,24},{44,28},{48,3... | collective-permute-start | bytes 24584 | tf_op jit(solution)/shard_map/ppermute | solution.py:494
  84.9 10.9 %collective-permute-start.15 = (f32[8,256]{1,0:T(8,128)S(1)}, f32[8,256]{1,0:T(8,128)S(1)}, u32[]{:S(2)}, u32[]{:S(2)}) collective-permute-start(f32[8,256]{1,0:T(8,128)S(1)} %get-tuple-element.34.st0), channel_id=1, source_target_pairs={{24,0},{28,4},{32,8},{36,12},{40,16},{44,20},{48,24},{52,28},{56,3... | collective-permute-start | bytes 24584 | tf_op jit(solution)/shard_map/ppermute | solution.py:494
  87.4 9.5 %collective-permute-start.16 = (f32[8,256]{1,0:T(8,128)S(1)}, f32[8,256]{1,0:T(8,128)S(1)}, u32[]{:S(2)}, u32[]{:S(2)}) collective-permute-start(f32[8,256]{1,0:T(8,128)S(1)} %get-tuple-element.34.st0), channel_id=1, source_target_pairs={{32,0},{36,4},{40,8},{44,12},{48,16},{52,20},{56,24},{60,28},{64,3... | collective-permute-start | bytes 24584 | tf_op jit(solution)/shard_map/ppermute | solution.py:494
  91.3 11.3 %all-to-all-start.1 = ((bf16[8,64,128]{2,1,0:T(8,128)(2,1)}), bf16[8,64,128]{2,1,0:T(8,128)(2,1)S(1)}, u32[]{:S(2)}, u32[]{:S(2)}) async-start(bf16[8,64,128]{2,1,0:T(8,128)(2,1)} %chain_walk.1), calls=%async_computation.1 | async-start | bytes 262144 | tf_op jit(solution)/shard_map/all_to_all | solution.py:476
  (24 other events, 167.3 us)
